TPU v7x, 512 devices: a whole 4x8x8 slice. The times are simulated.
512 devices in a mesh: seq: 64 (over y, z_hi, core), res: 8 (over z_lo, x).
Axes of the slice: x: 4, y: 8, z: 8 (z_hi: 4, z_lo: 2; z = z_hi * 2 + z_lo), core: 2. Of those that a mesh axis runs over, the one named last changes fastest.
Arguments:
- alignment_embedding: float32 [64, 1024, 256], P('seq', 'res'), may hold values from -2 to 2
- residue_couple_embedding: float32 [1024, 1024, 128], P('seq', 'res'), may hold values from -6 to 6
- couple_offset_matrix: float32 [128, 8], replicated, may hold values from -0.5 to 0.5
- horizontal_asker_matrix: bfloat16 [256, 256], replicated, may hold values from -24 to 24
- horizontal_lookup_matrix: bfloat16 [256, 256], replicated, may hold values from -24 to 24
- horizontal_content_matrix: bfloat16 [256, 256], replicated, may hold values from -0.375 to 0.375
- horizontal_sigmoid_matrix: bfloat16 [256, 256], replicated, may hold values from -0.375 to 0.375
- horizontal_final_matrix: bfloat16 [256, 256], replicated, may hold values from -1 to 1
- vertical_asker_matrix: bfloat16 [256, 256], replicated, may hold values from -24 to 24
- vertical_lookup_matrix: bfloat16 [256, 256], replicated, may hold values from -24 to 24
- vertical_content_matrix: bfloat16 [256, 256], replicated, may hold values from -0.375 to 0.375
- vertical_sigmoid_matrix: bfloat16 [256, 256], replicated, may hold values from -0.375 to 0.375
- vertical_final_matrix: bfloat16 [256, 256], replicated, may hold values from -1 to 1
Outputs:
- msa_out: float32 [64, 1024, 256], P('seq', 'res')
All inputs are finite; a program needn't handle non-finite values.
Results may differ from a plain program's by a relative error of at most 0.023.
Values may be sent and summed in bfloat16 or wider, within the bound.
No kernel may reach another device: no remote copies, remote signals or barrier semaphores. Data moves between devices by JAX's collectives and lax.ppermute only.
A program may use at most 64 MiB of HBM per device.

v0:
```python
import jax
import jax.numpy as jnp
from jax import lax
from jax.sharding import PartitionSpec as P

EPS = 1e-05


def standardize_features(inputs):
    centre = jnp.mean(inputs, axis=-1, keepdims=True)
    spread = jnp.mean(jnp.square(inputs - centre), axis=-1, keepdims=True)
    return (inputs - centre) * lax.rsqrt(spread + EPS)


def project(token_rows, weight):
    return jnp.dot(token_rows, weight, preferred_element_type=jnp.float32).astype(jnp.bfloat16)


def shards(
    alignment_embedding,
    residue_couple_embedding,
    couple_offset_matrix,
    horizontal_asker_matrix,
    horizontal_lookup_matrix,
    horizontal_content_matrix,
    horizontal_sigmoid_matrix,
    horizontal_final_matrix,
    vertical_asker_matrix,
    vertical_lookup_matrix,
    vertical_content_matrix,
    vertical_sigmoid_matrix,
    vertical_final_matrix,
):
    head_count = couple_offset_matrix.shape[1]
    homologs_each_shard, aminos_each_shard, feature_total = alignment_embedding.shape
    head_size = feature_total // head_count
    score_scale = head_size ** (-0.5)
    seq_devices = lax.axis_size("seq")
    residue_block = aminos_each_shard // seq_devices
    pair_normed = standardize_features(residue_couple_embedding)
    local_bias = jnp.einsum(
        "ijc,ch->hij", pair_normed, couple_offset_matrix, precision=lax.Precision.HIGHEST
    ).astype(jnp.bfloat16)
    column_bias = lax.all_gather(local_bias, "seq", axis=1, tiled=True)
    bias_rows = lax.all_to_all(column_bias, "res", split_axis=1, concat_axis=2, tiled=True)
    standardized_source = standardize_features(alignment_embedding).astype(jnp.bfloat16)
    token_rows = standardized_source.reshape(homologs_each_shard * aminos_each_shard, feature_total)
    queries = project(token_rows, horizontal_asker_matrix).reshape(
        homologs_each_shard, aminos_each_shard, head_count, head_size
    )
    gating = jax.nn.sigmoid(
        jnp.dot(token_rows, horizontal_sigmoid_matrix, preferred_element_type=jnp.float32)
    ).reshape(homologs_each_shard, aminos_each_shard, feature_total)
    initial = (
        jnp.full((homologs_each_shard, head_count, aminos_each_shard), -1e30, jnp.float32),
        jnp.zeros((homologs_each_shard, head_count, aminos_each_shard), jnp.float32),
        jnp.zeros((homologs_each_shard, head_count, aminos_each_shard, head_size), jnp.float32),
    )
    pieces = lax.all_gather(standardized_source, "res", axis=1, tiled=True)
    key_count = pieces.shape[1]
    piece_rows = pieces.reshape(homologs_each_shard * key_count, feature_total)
    key_rows = project(piece_rows, horizontal_lookup_matrix).reshape(
        homologs_each_shard, key_count, feature_total
    )
    value_rows = project(piece_rows, horizontal_content_matrix).reshape(
        homologs_each_shard, key_count, feature_total
    )
    key_count = key_rows.shape[1]
    key_heads = key_rows.reshape(homologs_each_shard, key_count, head_count, head_size)
    value_heads = value_rows.reshape(homologs_each_shard, key_count, head_count, head_size)
    bias_piece = bias_rows.astype(jnp.float32)

    def per_sequence(stacked):
        running_max, running_sum, weighted, query_seq, key_seq, value_seq = stacked
        logits = (
            jnp.einsum("qhd,khd->hqk", query_seq, key_seq, preferred_element_type=jnp.float32)
            * score_scale
            + bias_piece
        )
        new_max = jnp.maximum(running_max, jnp.max(logits, axis=-1))
        shrink = jnp.exp(running_max - new_max)
        exponents = jnp.exp(logits - new_max[..., None])
        running_sum = running_sum * shrink + jnp.sum(exponents, axis=-1)
        weights = exponents.astype(jnp.bfloat16)
        weighted = weighted * shrink[..., None] + jnp.einsum(
            "hqk,khd->hqd", weights, value_seq, preferred_element_type=jnp.float32
        )
        return (new_max, running_sum, weighted)

    final = lax.map(
        per_sequence, (initial[0], initial[1], initial[2], queries, key_heads, value_heads)
    )
    attended = final[2] / final[1][..., None]
    attended = jnp.transpose(attended, (0, 2, 1, 3)).reshape(
        homologs_each_shard, aminos_each_shard, feature_total
    )
    gated_rows = (gating * attended).astype(jnp.bfloat16)
    horizontal_mixing_delta = jnp.dot(
        gated_rows.reshape(-1, feature_total),
        horizontal_final_matrix,
        preferred_element_type=jnp.float32,
    )
    alignment_midway = alignment_embedding + horizontal_mixing_delta.reshape(
        homologs_each_shard, aminos_each_shard, feature_total
    )
    outgoing_raw = alignment_midway.reshape(
        homologs_each_shard, seq_devices, residue_block, feature_total
    )
    normed_block = standardize_features(
        lax.all_to_all(
            outgoing_raw.astype(jnp.bfloat16), "seq", split_axis=1, concat_axis=0, tiled=True
        ).astype(outgoing_raw.dtype)[:, 0]
    ).astype(jnp.bfloat16)
    seq_count = normed_block.shape[0]
    res_count = normed_block.shape[1]
    token_block = normed_block.reshape(seq_count * res_count, feature_total)
    query_block = project(token_block, vertical_asker_matrix).reshape(
        seq_count, res_count, head_count, head_size
    )
    key_block = project(token_block, vertical_lookup_matrix).reshape(
        seq_count, res_count, head_count, head_size
    )
    value_block = project(token_block, vertical_content_matrix).reshape(
        seq_count, res_count, head_count, head_size
    )
    gating_block = jax.nn.sigmoid(
        jnp.dot(token_block, vertical_sigmoid_matrix, preferred_element_type=jnp.float32)
    ).reshape(seq_count, res_count, feature_total)
    logits = (
        jnp.einsum("srhd,trhd->rhst", query_block, key_block, preferred_element_type=jnp.float32)
        * score_scale
    )
    row_max = jnp.max(logits, axis=-1, keepdims=True)
    exponents = jnp.exp(logits - row_max)
    denominator = jnp.sum(exponents, axis=-1)
    attended_block = jnp.einsum(
        "rhst,trhd->srhd",
        exponents.astype(jnp.bfloat16),
        value_block,
        preferred_element_type=jnp.float32,
    )
    attended_block = attended_block / jnp.transpose(denominator, (2, 0, 1))[..., None]
    gated_block = (
        gating_block * attended_block.reshape(seq_count, res_count, feature_total)
    ).astype(jnp.bfloat16)
    seq_count = gated_block.shape[0]
    res_count = gated_block.shape[1]
    update_rows = jnp.dot(
        gated_block.reshape(-1, feature_total),
        vertical_final_matrix,
        preferred_element_type=jnp.float32,
    )
    col_result = update_rows.reshape(seq_count, res_count, feature_total)[:, None]
    produced_result = lax.all_to_all(
        col_result.astype(jnp.bfloat16), "seq", split_axis=0, concat_axis=1, tiled=True
    ).astype(col_result.dtype)
    return alignment_midway + produced_result.reshape(
        homologs_each_shard, aminos_each_shard, feature_total
    )


def solution(mesh):
    in_specs = (
        P("seq", "res", None),
        P("seq", "res", None),
        P(),
        P(),
        P(),
        P(),
        P(),
        P(),
        P(),
        P(),
        P(),
        P(),
        P(),
    )
    out_specs = P("seq", "res", None)
    return jax.shard_map(shards, mesh=mesh, in_specs=in_specs, out_specs=out_specs, check_vma=False)
```

profile of v0, /device:TPU:1, one launch (start us, length us, event | category | flops | bytes accessed | tf_op | source)
XLA Modules:
  0.0 222.8 jit_solution(14909242464298797961)
XLA Ops:
  6.5 1.6 reduce_sum.75
  8.2 1.9 multiply_reduce_fusion
  10.1 3.3 %fusion.24 = bf16[8,16,128]{2,0,1:T(8,128)(2,1)} fusion(f32[16,128,128]{2,1,0:T(8,128)} %param.14, f32[16,128]{1,0:T(8,128)S(1)} %add_rsqrt_fusion.1, f32[16,128]{1,0:T(8,128)S(1)} %broadcast_multiply_fusion.1, f32[128,8]{0,1:T(8,128)} %param.15), kind=kOutput, calls=%fused_computation.35 | convolution fusion | flops 25706496 | bytes 1101824 | tf_op jit(solution)/shard_map/ijc,ch->hij/dot_general | solution.py:41
  13.3 91.0 %all-gather.2.cloned.1.call-done = bf16[8,1024,128]{2,0,1:T(8,128)(2,1)} async-done(((bf16[8,16,128]{2,0,1:T(8,128)(2,1)}), bf16[8,1024,128]{2,0,1:T(8,128)(2,1)}) %all-gather.2.cloned.1.call-update) | async-done | bytes 2097168 | tf_op jit(solution)/shard_map/all_gather | solution.py:44
  104.3 4.1 %all-to-all-start = ((bf16[8,1024,128]{2,0,1:T(8,128)(2,1)}), bf16[8,1024,128]{2,0,1:T(8,128)(2,1)S(1)}, u32[]{:S(2)}, u32[]{:S(2)}) async-start(bf16[8,1024,128]{2,0,1:T(8,128)(2,1)} %all-gather.2.cloned.1.call-done), calls=%async_computation | async-start | bytes 4194304 | tf_op jit(solution)/shard_map/all_to_all | solution.py:45
  108.5 0.2 multiply_reduce_fusion.1
  108.8 0.2 convolution_convert_fusion.6
  109.1 44.0 %all_gather.6 = bf16[1,1024,256]{2,1,0:T(8,128)(2,1)S(1)} all-gather(bf16[1,128,256]{2,1,0:T(8,128)(2,1)S(1)} %multiply_convert_fusion.1), channel_id=1, replica_groups=mesh['seq'=64,'res'=8] {'res'}, dimensions={1}, use_global_device_ids=true | all-gather | bytes 589824 | tf_op jit(solution)/shard_map/all_gather | solution.py:59
  153.1 0.3 convolution_convert_fusion
  153.4 1.2 convolution_convert_fusion.1
  154.7 3.1 %copy.70 = f32[8,8,128,128]{3,1,2,0:T(8,128)} copy(bf16[8,8,128,128]{3,0,2,1:T(8,128)(2,1)S(1)} %bitcast.75) | data formatting | bytes 6291456 | tf_op jit(solution)/shard_map/convert_element_type | solution.py:71
  157.9 4.9 %reshape.179 = f32[8,128,1024]{2,1,0:T(8,128)} reshape(f32[8,128,8,128]{3,2,1,0:T(8,128)} %bitcast.74) | data formatting | bytes 8388608 | tf_op jit(solution)/shard_map/convert_element_type | solution.py:71
  162.8 3.0 %fusion.49 = (f32[8,128]{1,0:T(8,128)S(1)}, f32[8,128,1024]{2,1,0:T(8,128)S(1)}) fusion(f32[8,128,1024]{2,1,0:T(8,128)} %reshape.179, bf16[128,8,32]{0,2,1:T(8,128)(2,1)S(1)} %bitcast.79, bf16[1024,8,32]{0,2,1:T(8,128)(2,1)S(1)} %bitcast.76), kind=kOutput, calls=%fused_computation.73 | convolution fusion | flops 70253568 | bytes 8982528 | tf_op jit(solution)/shard_map/while/body/eval_jaxpr/qhd,khd->hqk/dot_general | solution.py:76
  165.8 1.1 fusion
  167.0 0.9 fusion.9
  168.1 0.3 fusion.50
  168.4 27.1 %all_to_all.12 = bf16[1,64,2,256]{3,2,0,1:T(2,128)(2,1)S(1)} all-to-all(bf16[1,64,2,256]{3,2,0,1:T(2,128)(2,1)S(1)} %bitcast.80), channel_id=1, replica_groups=mesh['seq'=64,'res'=8] {'seq'}, dimensions={1} | all-to-all | bytes 131072 | tf_op jit(solution)/shard_map/all_to_all | solution.py:110
  195.9 0.2 fusion.40
  196.4 0.2 convolution_convert_fusion.3
  196.6 0.2 reshape.177
  196.8 0.2 convolution_convert_fusion.4
  196.9 0.2 reshape.176
  197.1 0.2 convolution_convert_fusion.5
  197.3 0.2 reshape.175
  197.5 0.3 fusion.53
  197.9 0.3 fusion.5
  198.1 0.3 copy.53
  198.4 0.2 reshape.178
  198.6 0.2 fusion.21
  198.9 0.2 fusion.23
  199.1 16.1 %all_to_all.13 = bf16[64,1,2,256]{3,2,1,0:T(2,128)(2,1)S(1)} all-to-all(bf16[64,1,2,256]{3,2,1,0:T(2,128)(2,1)S(1)} %copy.55), channel_id=1, replica_groups=mesh['seq'=64,'res'=8] {'seq'}, dimensions={0} | all-to-all | bytes 131072 | tf_op jit(solution)/shard_map/all_to_all | solution.py:154
  215.3 0.7 add.76
  (45 shorter events, 1.4 us)
Async XLA Ops:
  6.5 146.6 %copy-start = (bf16[256,256]{1,0:T(8,128)(2,1)S(1)}, bf16[256,256]{1,0:T(8,128)(2,1)}, u32[]{:S(2)}) copy-start(bf16[256,256]{1,0:T(8,128)(2,1)} %param.18) | copy-start | bytes 393220
  6.5 101.9 %copy-start.1 = (f32[1,128,256]{2,1,0:T(8,128)S(1)}, f32[1,128,256]{2,1,0:T(8,128)}, u32[]{:S(2)}) copy-start(f32[1,128,256]{2,1,0:T(8,128)} %param.13) | copy-start | bytes 393220
  6.5 102.3 %copy-start.2 = (bf16[256,256]{1,0:T(8,128)(2,1)S(1)}, bf16[256,256]{1,0:T(8,128)(2,1)}, u32[]{:S(2)}) copy-start(bf16[256,256]{1,0:T(8,128)(2,1)} %param.16) | copy-start | bytes 393220
  6.5 97.8 %all-gather.2.cloned.1.call-start = ((), (), s32[]{:S(2)}) async-start(), calls=%async_computation.3 | async-start | bytes 2129920 | tf_op jit(solution)/shard_map/all_gather | solution.py:44
  104.3 50.4 %all-to-all-start = ((bf16[8,1024,128]{2,0,1:T(8,128)(2,1)}), bf16[8,1024,128]{2,0,1:T(8,128)(2,1)S(1)}, u32[]{:S(2)}, u32[]{:S(2)}) async-start(bf16[8,1024,128]{2,0,1:T(8,128)(2,1)} %all-gather.2.cloned.1.call-done), calls=%async_computation | async-start | bytes 4194304 | tf_op jit(solution)/shard_map/all_to_all | solution.py:45
  165.8 2.2 %copy-start.7 = (bf16[256,256]{1,0:T(8,128)(2,1)S(1)}, bf16[256,256]{1,0:T(8,128)(2,1)}, u32[]{:S(2)}) copy-start(bf16[256,256]{1,0:T(8,128)(2,1)} %param.20) | copy-start | bytes 393220
  165.8 2.2 %copy-start.8 = (bf16[256,256]{1,0:T(8,128)(2,1)S(1)}, bf16[256,256]{1,0:T(8,128)(2,1)}, u32[]{:S(2)}) copy-start(bf16[256,256]{1,0:T(8,128)(2,1)} %param.19) | copy-start | bytes 393220
  166.9 29.5 %copy-start.3 = (bf16[256,256]{1,0:T(8,128)(2,1)S(1)}, bf16[256,256]{1,0:T(8,128)(2,1)}, u32[]{:S(2)}) copy-start(bf16[256,256]{1,0:T(8,128)(2,1)} %param.22) | copy-start | bytes 393220
  167.0 29.8 %copy-start.4 = (bf16[256,256]{1,0:T(8,128)(2,1)S(1)}, bf16[256,256]{1,0:T(8,128)(2,1)}, u32[]{:S(2)}) copy-start(bf16[256,256]{1,0:T(8,128)(2,1)} %param.21) | copy-start | bytes 393220
  167.0 30.1 %copy-start.5 = (bf16[256,256]{1,0:T(8,128)(2,1)S(1)}, bf16[256,256]{1,0:T(8,128)(2,1)}, u32[]{:S(2)}) copy-start(bf16[256,256]{1,0:T(8,128)(2,1)} %param.23) | copy-start | bytes 393220
  167.9 30.7 %copy-start.9 = (bf16[256,256]{1,0:T(8,128)(2,1)S(1)}, bf16[256,256]{1,0:T(8,128)(2,1)}, u32[]{:S(2)}) copy-start(bf16[256,256]{1,0:T(8,128)(2,1)} %param.24) | copy-start | bytes 393220
  168.4 30.5 %copy-start.6 = (bf16[256,256]{1,0:T(8,128)(2,1)S(1)}, bf16[256,256]{1,0:T(8,128)(2,1)}, u32[]{:S(2)}) copy-start(bf16[256,256]{1,0:T(8,128)(2,1)} %param.25) | copy-start | bytes 393220
Sparse Core Ops, SparseCore 0:
  13.5 90.8 all-gather.1
where the time goes:
time: 223 us
  waiting for transfers between devices  91 us (41%)
  blocking collectives  87.3 us (39%)
  between operations  13.8 us (6%)
  matrix products  10.6 us (5%)
  local copies, waits for them, and re-layouts  9.75 us (4%)
  other arithmetic  6.28 us (3%)
  starting transfers between devices  4.08 us (2%)
    all_gather x1, waiting for transfers between devices, shards(): column_bias = lax.all_gather(local_bias, 'seq', axis=1, tiled=True)  91 us
    all_gather x1, blocking collectives, shards(): pieces = lax.all_gather(standardized_source, 'res', axis=1, tiled=True)  44 us
    all_to_all x1, blocking collectives, shards(): lax.all_to_all(outgoing_raw.astype(jnp.bfloat16), 'seq', split_axis=1, co...  27.1 us
    all_to_all x1, blocking collectives, shards(): lax.all_to_all(col_result.astype(jnp.bfloat16), 'seq', split_axis=0, conc...  16.1 us
    convert_element_type x2, local copies, waits for them, and re-layouts, shards(): bias_piece = bias_rows.astype(jnp.float32)  8.05 us
  transfers between devices with their start and end apart: 2, of which 1 were waited for; matrix products, arithmetic and copies ran while one was open for 1% of the time, Pallas kernels for 0%

commit v1 on v0

v1 whole, which is shorter than its diff:
```python
import functools

import jax
import jax.numpy as jnp
from jax import lax
from jax.experimental import pallas as pl
from jax.experimental.pallas import tpu as pltpu
from jax.sharding import Mesh, PartitionSpec as P

EPS = 1e-05
HEADS = 8
HEAD_SIZE = 32
FEATURES = HEADS * HEAD_SIZE
SCALE = HEAD_SIZE ** (-0.5)
Y, ZH, C, ZL, X = 8, 4, 2, 2, 4
SEQ = ("y", "zh", "c")
RES = ("zl", "x")
CHIPS = Y * ZH
VMEM = pl.BlockSpec(memory_space=pltpu.VMEM)
SMEM = pl.BlockSpec(memory_space=pltpu.SMEM)
NT = (((1,), (1,)), ((), ()))
F32, BF16 = jnp.float32, jnp.bfloat16


def call(kernel, out_shape, *args, scratch=(), smem=0, flops=0, size=0, vmem=48):
    return pl.pallas_call(
        kernel,
        out_shape=out_shape,
        in_specs=[SMEM] * smem + [VMEM] * (len(args) - smem),
        out_specs=jax.tree.map(lambda _: VMEM, out_shape),
        scratch_shapes=list(scratch),
        compiler_params=pltpu.CompilerParams(vmem_limit_bytes=vmem * 2**20),
        cost_estimate=pl.CostEstimate(flops=flops, bytes_accessed=size, transcendentals=0),
    )(*args)


def standardize(rows):
    centre = jnp.mean(rows, axis=-1, keepdims=True)
    moved = rows - centre
    spread = jnp.mean(moved * moved, axis=-1, keepdims=True)
    return moved * lax.rsqrt(spread + EPS)


def matmul(a, b):
    return jnp.dot(a, b, preferred_element_type=F32)


def head_mask(shape, head):
    lane = lax.broadcasted_iota(jnp.int32, shape, 1)
    return (lane >= head * HEAD_SIZE) & (lane < (head + 1) * HEAD_SIZE)


def pair_kernel(x_ref, w_ref, out_ref, scr):
    w = w_ref[...]
    wh = w.astype(BF16)
    wl = (w - wh.astype(F32)).astype(BF16)
    top = jnp.concatenate([wh.astype(F32), wh.astype(F32)], axis=1)
    low = jnp.concatenate([wl.astype(F32), jnp.zeros_like(w)], axis=1)
    weights = jnp.concatenate([top, low], axis=0).astype(BF16)
    for i in range(x_ref.shape[0]):
        d = standardize(x_ref[i])
        dh = d.astype(BF16)
        dl = (d - dh.astype(F32)).astype(BF16)
        both = jnp.concatenate([dh, dl], axis=1)
        part = lax.dot_general(weights, both, NT, preferred_element_type=F32)
        scr[:, i, :] = part[:HEADS] + part[HEADS:]
    out_ref[...] = scr[...].astype(BF16)


def norm_kernel(x_ref, out_ref):
    block = standardize(x_ref[...]).astype(BF16)
    for i in range(out_ref.shape[0]):
        out_ref[i] = block


def project_kernel(own_ref, pair_ref, rows_ref, wq_ref, wk_ref, wv_ref, wg_ref, q_ref, k_ref, v_ref, g_ref):
    for s, ref in enumerate((own_ref, pair_ref)):
        tokens = ref[...]
        k_ref[s] = matmul(tokens, wk_ref[...]).astype(BF16)
        v_ref[s] = matmul(tokens, wv_ref[...]).astype(BF16)
    count = rows_ref.shape[1]
    tokens = standardize(rows_ref[...].reshape(2 * count, FEATURES)).astype(BF16)
    g_ref[...] = jax.nn.sigmoid(matmul(tokens, wg_ref[...])).reshape(2, count, FEATURES)
    q = matmul(tokens, wq_ref[...])
    for h in range(HEADS):
        masked = jnp.where(head_mask(q.shape, h), q, 0.0).astype(BF16)
        q_ref[:, h * count : (h + 1) * count, :] = masked.reshape(2, count, FEATURES)


def row_kernel(c_ref, bias_ref, q_ref, k_ref, v_ref, g_ref, rows_ref, wo_ref, mid_ref, send_ref, s_scr, p_scr, t_scr):
    count = rows_ref.shape[1]
    keys = k_ref.shape[1]
    cols = keys // Y
    gated = []
    for s in range(2):
        s_scr[s] = lax.dot_general(q_ref[s], k_ref[s], NT, preferred_element_type=F32)
    for s in range(2):
        sums = []
        for h in range(HEADS):
            lo, hi = h * count, (h + 1) * count
            logits = []
            for y in range(Y):
                bias = bias_ref[y * ZH : (y + 1) * ZH, h].astype(F32).reshape(count, cols)
                logits.append(s_scr[s, lo:hi, y * cols : (y + 1) * cols] * SCALE + bias)
            top = functools.reduce(jnp.maximum, logits)
            top = jnp.max(top, axis=-1, keepdims=True)
            total = None
            for y in range(Y):
                e = jnp.exp(logits[y] - top)
                total = e if total is None else total + e
                p_scr[s, lo:hi, y * cols : (y + 1) * cols] = e.astype(BF16)
            sums.append(jnp.sum(total, axis=-1, keepdims=True))
        out = matmul(p_scr[s], v_ref[s])
        attended = jnp.zeros((count, FEATURES), F32)
        for h in range(HEADS):
            attended = jnp.where(
                head_mask(attended.shape, h), out[h * count : (h + 1) * count] / sums[h], attended
            )
        gated.append((g_ref[s] * attended).astype(BF16))
    delta = matmul(jnp.concatenate(gated, axis=0), wo_ref[...])
    mids = [rows_ref[s] + delta[s * count : (s + 1) * count] for s in range(2)]
    normed = []
    for s in range(2):
        mid_ref[s] = mids[s]
        normed.append(standardize(mids[s]))
    first = c_ref[0] == 0
    ordered = [jnp.where(first, normed[0], normed[1]), jnp.where(first, normed[1], normed[0])]
    for s in range(2):
        for rr in range(2):
            for half in range(2):
                block = ordered[s][rr * CHIPS : (rr + 1) * CHIPS, half * 128 : (half + 1) * 128]
                t_scr[pl.ds(s * 4 + rr * 2 + half, CHIPS, stride=8), :] = block
    send_ref[...] = t_scr[...].reshape(CHIPS, 8, 128).astype(BF16)


def column_kernel(x_ref, wq_ref, wk_ref, wv_ref, wg_ref, out_ref, t_scr):
    t_scr[...] = x_ref[...].astype(F32).reshape(CHIPS * 8, 128)
    part = [t_scr[pl.ds(i, CHIPS, stride=8), :] for i in range(8)]
    count = 2 * CHIPS
    tokens = jnp.concatenate(
        [
            jnp.concatenate([part[s * 4 + rr * 2], part[s * 4 + rr * 2 + 1]], axis=1)
            for rr in range(2)
            for s in range(2)
        ],
        axis=0,
    ).astype(BF16)
    q = matmul(tokens, wq_ref[...])
    k = matmul(tokens, wk_ref[...]).astype(BF16)
    v = matmul(tokens, wv_ref[...]).astype(BF16)
    g = jax.nn.sigmoid(matmul(tokens, wg_ref[...]))
    for rr in range(2):
        lo, hi = rr * count, (rr + 1) * count
        masked = jnp.concatenate(
            [jnp.where(head_mask((count, FEATURES), h), q[lo:hi], 0.0) for h in range(HEADS)], axis=0
        ).astype(BF16)
        logits = lax.dot_general(masked, k[lo:hi], NT, preferred_element_type=F32) * SCALE
        e = jnp.exp(logits - jnp.max(logits, axis=-1, keepdims=True))
        total = jnp.sum(e, axis=-1, keepdims=True)
        out = matmul(e.astype(BF16), v[lo:hi]) / total
        attended = jnp.zeros((count, FEATURES), F32)
        for h in range(HEADS):
            attended = jnp.where(
                head_mask(attended.shape, h), out[h * count : (h + 1) * count], attended
            )
        gated = g[lo:hi] * attended
        for s in range(2):
            for half in range(2):
                t_scr[pl.ds(s * 4 + rr * 2 + half, CHIPS, stride=8), :] = gated[
                    s * CHIPS : (s + 1) * CHIPS, half * 128 : (half + 1) * 128
                ]
    out_ref[...] = t_scr[...].reshape(CHIPS, 8, 128).astype(BF16)


def final_kernel(c_ref, x_ref, own_ref, pair_ref, wo_ref, out_ref, t_scr):
    t_scr[...] = x_ref[...].astype(F32).reshape(CHIPS * 8, 128)
    part = [t_scr[pl.ds(i, CHIPS, stride=8), :] for i in range(8)]
    tokens = jnp.concatenate(
        [
            jnp.concatenate([part[s * 4 + rr * 2], part[s * 4 + rr * 2 + 1]], axis=1)
            for s in range(2)
            for rr in range(2)
        ],
        axis=0,
    ).astype(BF16)
    update = matmul(tokens, wo_ref[...])
    first = c_ref[0] == 0
    own, pair = own_ref[...], pair_ref[...]
    middle = [jnp.where(first, own, pair), jnp.where(first, pair, own)]
    count = own.shape[0]
    step = count // ZH
    for s in range(2):
        result = middle[s] + update[s * count : (s + 1) * count]
        for z in range(ZH):
            at = (z * 2 + s) * step
            out_ref[at : at + step] = result[z * step : (z + 1) * step]


def shards(
    alignment,
    pair,
    offset_matrix,
    row_wq,
    row_wk,
    row_wv,
    row_wg,
    row_wo,
    col_wq,
    col_wk,
    col_wv,
    col_wg,
    col_wo,
):
    core = lax.axis_index("c")
    core_ref = core.astype(jnp.int32).reshape(1)
    tokens = alignment.shape[1]
    half = tokens // 2
    swap = [(0, 1), (1, 0)]
    turn = [(a * 8 + b, b * 8 + a) for a in range(8) for b in range(8)]

    bias = call(
        pair_kernel,
        jax.ShapeDtypeStruct((HEADS, pair.shape[0], pair.shape[1]), BF16),
        pair,
        offset_matrix.T,
        scratch=[pltpu.VMEM((HEADS, pair.shape[0], pair.shape[1]), F32)],
    )
    bias = lax.ppermute(bias, ("y", "zl", "x"), turn)

    rows = alignment[0].reshape(ZH, 2, half // ZH, FEATURES)
    mine = jnp.where(core == 0, rows[:, 0], rows[:, 1]).reshape(half, FEATURES)
    other = jnp.where(core == 0, rows[:, 1], rows[:, 0]).reshape(half, FEATURES)
    other = lax.ppermute(other, "c", swap)
    query_rows = jnp.stack([mine, other])

    spread = call(
        norm_kernel, jax.ShapeDtypeStruct((8, tokens, FEATURES), BF16), alignment[0]
    )
    own_normed = lax.all_to_all(spread, RES, 0, 0, tiled=True).reshape(8 * tokens, FEATURES)
    pair_normed = lax.ppermute(own_normed, "c", swap)

    wide = jnp.broadcast_to(bias[None], (CHIPS,) + bias.shape)
    wide = lax.all_to_all(wide, ("y", "zh"), 0, 0, tiled=True)

    keys = 8 * tokens
    q, k, v, g = call(
        project_kernel,
        (
            jax.ShapeDtypeStruct((2, HEADS * half, FEATURES), BF16),
            jax.ShapeDtypeStruct((2, keys, FEATURES), BF16),
            jax.ShapeDtypeStruct((2, keys, FEATURES), BF16),
            jax.ShapeDtypeStruct((2, half, FEATURES), F32),
        ),
        own_normed,
        pair_normed,
        query_rows,
        row_wq,
        row_wk,
        row_wv,
        row_wg,
        flops=2 * 2 * keys * FEATURES * 2 * FEATURES,
        size=4 * 2**20,
    )
    middle, send = call(
        row_kernel,
        (
            jax.ShapeDtypeStruct((2, half, FEATURES), F32),
            jax.ShapeDtypeStruct((CHIPS, 8, 128), BF16),
        ),
        core_ref,
        wide,
        q,
        k,
        v,
        g,
        query_rows,
        row_wo,
        smem=1,
        scratch=[
            pltpu.VMEM((2, HEADS * half, keys), F32),
            pltpu.VMEM((2, HEADS * half, keys), BF16),
            pltpu.VMEM((CHIPS * 8, 128), F32),
        ],
        flops=2 * 2 * 2 * HEADS * half * keys * FEATURES,
        size=6 * 2**20,
    )
    middle_pair = lax.ppermute(middle[1], "c", swap)

    block = lax.all_to_all(send, ("y", "zh"), 0, 0, tiled=True)
    gated = call(
        column_kernel,
        jax.ShapeDtypeStruct((CHIPS, 8, 128), BF16),
        block,
        col_wq,
        col_wk,
        col_wv,
        col_wg,
        scratch=[pltpu.VMEM((CHIPS * 8, 128), F32)],
    )
    back = lax.all_to_all(gated.reshape(2 * CHIPS, 4, 128), SEQ, 0, 0, tiled=True)
    out = call(
        final_kernel,
        jax.ShapeDtypeStruct((tokens, FEATURES), F32),
        core_ref,
        back.reshape(CHIPS, 8, 128),
        middle[0],
        middle_pair,
        col_wo,
        smem=1,
        scratch=[pltpu.VMEM((CHIPS * 8, 128), F32)],
    )
    return out[None]


def solution(mesh):
    fine = Mesh(mesh.devices.reshape(Y, ZH, C, ZL, X), ("y", "zh", "c", "zl", "x"))
    split = P(SEQ, RES, None)
    in_specs = (split, split) + (P(),) * 11
    return jax.shard_map(shards, mesh=fine, in_specs=in_specs, out_specs=split, check_vma=False)
```

time: 223 us -> 108 us (0.48)
  blocking collectives: 87.3 us -> 19.4 us
  waiting for transfers between devices: 91 us -> 28.3 us
  starting transfers between devices: 4.08 us -> 42.1 us
  between operations: 13.8 us -> 0.23 us
  matrix products: 10.6 us -> 0 us
  Pallas kernels: 0 us -> 7.31 us
  other arithmetic: 6.28 us -> 0.02 us
    all_gather x1 -> x0, waiting for transfers between devices: 91 us -> none  [shards(): column_bias = lax.all_gather(local_bias, 'seq', axis=1, tiled=True)]
    all_gather x1 -> x0, blocking collectives: 44 us -> none  [shards(): pieces = lax.all_gather(standardized_source, 'res', axis=1, tiled=True)]
    all_to_all x1 -> x3, starting transfers between devices: 4.08 us -> 32.5 us  [the longest x1 18.2 us: shards(): wide = lax.all_to_all(wide, ('y', 'zh'), 0, 0, tiled=True)]
    all_to_all x1 -> x3, waiting for transfers between devices: 0.01 us -> 26.2 us  [the longest x1 11.7 us: shards(): wide = lax.all_to_all(wide, ('y', 'zh'), 0, 0, tiled=True)]
    all_to_all x2 -> x1, blocking collectives: 43.3 us -> 19.4 us  [shards(): block = lax.all_to_all(send, ('y', 'zh'), 0, 0, tiled=True)]
    dot_general x14 -> x0, matrix products: 10.6 us -> none  [the longest x1 3.25 us: shards(): jnp.einsum('ijc,ch->hij', pair_normed, couple_offset_matrix, precision=la...]
    ppermute x0 -> x4, starting transfers between devices: none -> 9.61 us  [the longest x1 4.28 us: shards(): pair_normed = lax.ppermute(own_normed, 'c', swap)]
    unnamed x20 -> x44, local copies, waits for them, and re-layouts: 0.06 us -> 8.96 us
  transfers between devices with their start and end apart: 2 -> 7, of which waited for: 1 -> 5; matrix products, arithmetic and copies ran while one was open for 1% -> 0% of each run, Pallas kernels for 0% -> 2%
where the time goes in v1:
time: 108 us
  starting transfers between devices  42.1 us (39%)
  waiting for transfers between devices  28.3 us (26%)
  blocking collectives  19.4 us (18%)
  local copies, waits for them, and re-layouts  10.2 us (9%)
  Pallas kernels  7.31 us (7%)
    all_to_all x1, blocking collectives, shards(): block = lax.all_to_all(send, ('y', 'zh'), 0, 0, tiled=True)  19.4 us
    all_to_all x1, starting transfers between devices, shards(): wide = lax.all_to_all(wide, ('y', 'zh'), 0, 0, tiled=True)  18.2 us
    all_to_all x1, waiting for transfers between devices, shards(): wide = lax.all_to_all(wide, ('y', 'zh'), 0, 0, tiled=True)  11.7 us
    all_to_all x1, waiting for transfers between devices, shards(): lax.all_to_all(gated.reshape(2 * CHIPS, 4, 128), SEQ, 0, 0, tiled=True)  9 us
    unnamed x44, local copies, waits for them, and re-layouts  8.96 us
    all_to_all x1, starting transfers between devices, shards(): lax.all_to_all(gated.reshape(2 * CHIPS, 4, 128), SEQ, 0, 0, tiled=True)  7.51 us
    pallas_call x6, Pallas kernels, call(): pl.pallas_call(kernel, out_shape=out_shape, in_specs=[SMEM] * smem + [VME...  7.31 us
    all_to_all x1, starting transfers between devices, shards(): lax.all_to_all(spread, RES, 0, 0, tiled=True).reshape(8 * tokens, FEATURES)  6.79 us
  transfers between devices with their start and end apart: 7, of which 5 were waited for; matrix products, arithmetic and copies ran while one was open for 0% of the time, Pallas kernels for 2%

profile of v1, /device:TPU:1, one launch (start us, length us, event | category | flops | bytes accessed | tf_op | source)
XLA Modules:
  0.0 107.6 jit_solution(2380253847369172784)
XLA Ops:
  0.0 1.0 copy-done.3
  1.0 1.0 shard_map.128
  2.0 6.8 %all-to-all-start.1 = ((bf16[8,128,256]{2,1,0:T(8,128)(2,1)}), bf16[8,128,256]{2,1,0:T(8,128)(2,1)S(1)}, u32[]{:S(2)}, u32[]{:S(2)}) async-start(bf16[8,128,256]{2,1,0:T(8,128)(2,1)} %shard_map.128), calls=%async_computation.1 | async-start | bytes 1048576 | tf_op jit(solution)/shard_map/all_to_all | solution.py:239
  8.8 0.9 shard_map.127
  9.7 0.7 collective-permute-start
  10.4 5.5 %all-to-all-done.1 = bf16[8,128,256]{2,1,0:T(8,128)(2,1)S(1)} async-done(((bf16[8,128,256]{2,1,0:T(8,128)(2,1)}), bf16[8,128,256]{2,1,0:T(8,128)(2,1)S(1)}, u32[]{:S(2)}, u32[]{:S(2)}) %all-to-all-start.1) | async-done | bytes 524320 | tf_op jit(solution)/shard_map/all_to_all | solution.py:239
  15.9 1.2 %broadcast_in_dim.4 = bf16[32,8,16,128]{3,2,1,0:T(8,128)(2,1)} broadcast(bf16[8,16,128]{2,1,0:T(8,128)(2,1)S(1)} %collective-permute-done), dimensions={1,2,3} | broadcast | bytes 1081344 | tf_op jit(solution)/shard_map/broadcast_in_dim | solution.py:242
  17.1 18.2 %all-to-all-start = ((bf16[32,8,16,128]{3,2,1,0:T(8,128)(2,1)}), bf16[32,8,16,128]{3,2,1,0:T(8,128)(2,1)S(1)}, u32[]{:S(2)}, u32[]{:S(2)}) async-start(bf16[32,8,16,128]{3,2,1,0:T(8,128)(2,1)} %broadcast_in_dim.4), calls=%async_computation | async-start | bytes 2097152 | tf_op jit(solution)/shard_map/all_to_all | solution.py:243
  35.4 4.3 %collective-permute-start.1 = (bf16[1024,256]{1,0:T(8,128)(2,1)S(1)}, bf16[1024,256]{1,0:T(8,128)(2,1)S(1)}, u32[]{:S(2)}, u32[]{:S(2)}) collective-permute-start(bf16[1024,256]{1,0:T(8,128)(2,1)S(1)} %bitcast.29), channel_id=1, source_target_pairs={{0,8},{8,0},{1,9},{9,1},{2,10},{10,2},{3,11},{11,3},{4,12},{12,4},... | collective-permute-start | bytes 1572872 | tf_op jit(solution)/shard_map/ppermute | solution.py:240
  39.7 2.1 %collective-permute-start.2 = (f32[64,256]{1,0:T(8,128)S(1)}, f32[64,256]{1,0:T(8,128)S(1)}, u32[]{:S(2)}, u32[]{:S(2)}) collective-permute-start(f32[64,256]{1,0:T(8,128)S(1)} %bitcast.34), channel_id=1, source_target_pairs={{0,8},{8,0},{1,9},{9,1},{2,10},{10,2},{3,11},{11,3},{4,12},{12,4},... | collective-permute-start | bytes 196616 | tf_op jit(solution)/shard_map/ppermute | solution.py:233
  41.8 1.2 %collective-permute-done.2 = f32[64,256]{1,0:T(8,128)S(1)} collective-permute-done((f32[64,256]{1,0:T(8,128)S(1)}, f32[64,256]{1,0:T(8,128)S(1)}, u32[]{:S(2)}, u32[]{:S(2)}) %collective-permute-start.2) | collective-permute-done | bytes 65568 | tf_op jit(solution)/shard_map/ppermute | solution.py:233
  43.0 0.0 copy-start.7
  43.0 0.8 copy-done.16
  43.8 1.0 copy-done.17
  44.9 0.9 copy-done.18
  45.8 0.9 copy-done.19
  46.7 0.9 copy-done.20
  47.6 0.9 copy-done.21
  48.5 0.8 shard_map.129
  49.3 0.8 copy-done.1
  50.0 11.7 %all-to-all-done.bias_ref = bf16[32,8,16,128]{3,2,1,0:T(8,128)(2,1)S(1)} async-done(((bf16[32,8,16,128]{3,2,1,0:T(8,128)(2,1)}), bf16[32,8,16,128]{3,2,1,0:T(8,128)(2,1)S(1)}, u32[]{:S(2)}, u32[]{:S(2)}) %all-to-all-start) | async-done | bytes 1048608 | tf_op jit(solution)/shard_map/all_to_all | solution.py:243
  61.8 1.0 copy-done.2
  62.8 2.4 %shard_map.130 = (f32[2,64,256]{2,1,0:T(8,128)S(1)}, bf16[32,8,128]{2,1,0:T(8,128)(2,1)S(1)}) custom-call(s32[1]{0:T(128)} %bitcast.c_ref, bf16[32,8,16,128]{3,2,1,0:T(8,128)(2,1)S(1)} %all-to-all-done.bias_ref, bf16[2,512,256]{2,1,0:T(8,128)(2,1)S(1)} %copy-done.2, bf16[2,1024,256]{2,1,0:T(8,128)(2,1)S(1)} %get-tuple-element.12.k_ref, ...), custom_call_target="tpu_custom_call" | custom-call | flops 1073741824 | bytes 6291456 | tf_op jit(solution)/shard_map/pallas_call | solution.py:26
  65.2 0.6 copy-done.12
  65.9 19.4 %all_to_all.20.x_ref = bf16[32,8,128]{2,1,0:T(8,128)(2,1)S(1)} all-to-all(bf16[32,8,128]{2,1,0:T(8,128)(2,1)S(1)} %get-tuple-element.15), channel_id=1, replica_groups=mesh['y'=8,'zh'=4,'c'=2,'zl'=2,'x'=4] {'y','zh'}, dimensions={0} | all-to-all | bytes 131072 | tf_op jit(solution)/shard_map/all_to_all | solution.py:289
  85.3 1.4 %shard_map.131 = bf16[32,8,128]{2,1,0:T(8,128)(2,1)} custom-call(bf16[32,8,128]{2,1,0:T(8,128)(2,1)S(1)} %all_to_all.20.x_ref, bf16[256,256]{1,0:T(8,128)(2,1)S(1)} %copy-done.8, bf16[256,256]{1,0:T(8,128)(2,1)S(1)} %copy-done.9, bf16[256,256]{1,0:T(8,128)(2,1)S(1)} %copy-done.10, bf16[256,256]{1,0:T(8,128)(2,1)S(1)} %copy-done.11), custom_call_target="tpu_custom_call" | custom-call | tf_op jit(solution)/shard_map/pallas_call | solution.py:26
  86.7 7.5 %all-to-all-start.3 = ((bf16[64,4,128]{2,1,0:T(4,128)(2,1)}), bf16[64,4,128]{2,1,0:T(4,128)(2,1)S(1)}, u32[]{:S(2)}, u32[]{:S(2)}) async-start(bf16[64,4,128]{2,1,0:T(4,128)(2,1)} %bitcast.8), calls=%async_computation.3 | async-start | bytes 131072 | tf_op jit(solution)/shard_map/all_to_all | solution.py:300
  94.3 0.0 copy-start.14
  94.3 2.6 %collective-permute-start.3 = (f32[64,256]{1,0:T(8,128)S(1)}, f32[64,256]{1,0:T(8,128)S(1)}, u32[]{:S(2)}, u32[]{:S(2)}) collective-permute-start(f32[64,256]{1,0:T(8,128)S(1)} %get-tuple-element.17), channel_id=1, source_target_pairs={{0,8},{8,0},{1,9},{9,1},{2,10},{10,2},{3,11},{11,3},{4,12},{12,4},... | collective-permute-start | bytes 196616 | tf_op jit(solution)/shard_map/ppermute | solution.py:287
  96.9 0.9 collective-permute-done.3.pair_ref
  97.8 9.0 %all-to-all-done.3 = bf16[64,4,128]{2,1,0:T(4,128)(2,1)S(1)} async-done(((bf16[64,4,128]{2,1,0:T(4,128)(2,1)}), bf16[64,4,128]{2,1,0:T(4,128)(2,1)S(1)}, u32[]{:S(2)}, u32[]{:S(2)}) %all-to-all-start.3) | async-done | bytes 65568 | tf_op jit(solution)/shard_map/all_to_all | solution.py:300
  106.8 0.8 shard_map.132
  (37 shorter events, 0.1 us)
Async XLA Ops:
  0.0 8.8 %copy-start = (f32[16,128,128]{2,1,0:T(8,128)S(1)}, f32[16,128,128]{2,1,0:T(8,128)}, u32[]{:S(2)}) copy-start(f32[16,128,128]{2,1,0:T(8,128)} %x_ref.1) | copy-start | bytes 3145732
  0.0 1.0 copy-start.3
  2.0 6.8 %copy-start.15 = (f32[128,8]{0,1:T(8,128)S(1)}, f32[128,8]{0,1:T(8,128)}, u32[]{:S(2)}) copy-start(f32[128,8]{0,1:T(8,128)} %param.15) | copy-start | bytes 12292
  2.0 13.9 %all-to-all-start.1 = ((bf16[8,128,256]{2,1,0:T(8,128)(2,1)}), bf16[8,128,256]{2,1,0:T(8,128)(2,1)S(1)}, u32[]{:S(2)}, u32[]{:S(2)}) async-start(bf16[8,128,256]{2,1,0:T(8,128)(2,1)} %shard_map.128), calls=%async_computation.1 | async-start | bytes 1048576 | tf_op jit(solution)/shard_map/all_to_all | solution.py:239
  9.7 0.7 collective-permute-start
  15.9 19.5 %copy-start.5 = (bf16[8,128,256]{2,1,0:T(8,128)(2,1)}, bf16[8,128,256]{2,1,0:T(8,128)(2,1)S(1)}, u32[]{:S(2)}) copy-start(bf16[8,128,256]{2,1,0:T(8,128)(2,1)S(1)} %all-to-all-done.1) | copy-start | bytes 1572868
  17.1 22.5 %copy-start.4 = (f32[1,128,256]{2,1,0:T(8,128)S(1)}, f32[1,128,256]{2,1,0:T(8,128)}, u32[]{:S(2)}) copy-start(f32[1,128,256]{2,1,0:T(8,128)} %param.13) | copy-start | bytes 393220
  17.1 44.6 %all-to-all-start = ((bf16[32,8,16,128]{3,2,1,0:T(8,128)(2,1)}), bf16[32,8,16,128]{3,2,1,0:T(8,128)(2,1)S(1)}, u32[]{:S(2)}, u32[]{:S(2)}) async-start(bf16[32,8,16,128]{3,2,1,0:T(8,128)(2,1)} %broadcast_in_dim.4), calls=%async_computation | async-start | bytes 2097152 | tf_op jit(solution)/shard_map/all_to_all | solution.py:243
  35.4 7.6 %collective-permute-start.1 = (bf16[1024,256]{1,0:T(8,128)(2,1)S(1)}, bf16[1024,256]{1,0:T(8,128)(2,1)S(1)}, u32[]{:S(2)}, u32[]{:S(2)}) collective-permute-start(bf16[1024,256]{1,0:T(8,128)(2,1)S(1)} %bitcast.29), channel_id=1, source_target_pairs={{0,8},{8,0},{1,9},{9,1},{2,10},{10,2},{3,11},{11,3},{4,12},{12,4},... | collective-permute-start | bytes 1572872 | tf_op jit(solution)/shard_map/ppermute | solution.py:240
  39.7 4.2 %copy-start.6 = (bf16[8,128,256]{2,1,0:T(8,128)(2,1)S(1)}, bf16[8,128,256]{2,1,0:T(8,128)(2,1)}, u32[]{:S(2)}) copy-start(bf16[8,128,256]{2,1,0:T(8,128)(2,1)} %copy-done.5) | copy-start | bytes 1572868
  39.7 3.3 %collective-permute-start.2 = (f32[64,256]{1,0:T(8,128)S(1)}, f32[64,256]{1,0:T(8,128)S(1)}, u32[]{:S(2)}, u32[]{:S(2)}) collective-permute-start(f32[64,256]{1,0:T(8,128)S(1)} %bitcast.34), channel_id=1, source_target_pairs={{0,8},{8,0},{1,9},{9,1},{2,10},{10,2},{3,11},{11,3},{4,12},{12,4},... | collective-permute-start | bytes 196616 | tf_op jit(solution)/shard_map/ppermute | solution.py:233
  43.0 18.8 %copy-start.7 = (bf16[256,256]{1,0:T(8,128)(2,1)S(1)}, bf16[256,256]{1,0:T(8,128)(2,1)}, u32[]{:S(2)}) copy-start(bf16[256,256]{1,0:T(8,128)(2,1)} %wo_ref.2) | copy-start | bytes 393220
  43.0 0.8 copy-start.16
  43.8 1.0 copy-start.17
  44.9 0.9 copy-start.18
  45.8 0.9 copy-start.19
  46.7 0.9 copy-start.20
  47.6 0.9 copy-start.21
  49.2 0.8 copy-start.1
  61.8 1.0 copy-start.2
  62.8 22.5 %copy-start.9 = (bf16[256,256]{1,0:T(8,128)(2,1)S(1)}, bf16[256,256]{1,0:T(8,128)(2,1)}, u32[]{:S(2)}) copy-start(bf16[256,256]{1,0:T(8,128)(2,1)} %wk_ref.3) | copy-start | bytes 393220
  62.8 22.5 %copy-start.10 = (bf16[256,256]{1,0:T(8,128)(2,1)S(1)}, bf16[256,256]{1,0:T(8,128)(2,1)}, u32[]{:S(2)}) copy-start(bf16[256,256]{1,0:T(8,128)(2,1)} %wv_ref.3) | copy-start | bytes 393220
  62.8 22.5 %copy-start.11 = (bf16[256,256]{1,0:T(8,128)(2,1)S(1)}, bf16[256,256]{1,0:T(8,128)(2,1)}, u32[]{:S(2)}) copy-start(bf16[256,256]{1,0:T(8,128)(2,1)} %wg_ref.3) | copy-start | bytes 393220
  65.2 0.7 copy-start.12
  65.9 19.4 %copy-start.8 = (bf16[256,256]{1,0:T(8,128)(2,1)S(1)}, bf16[256,256]{1,0:T(8,128)(2,1)}, u32[]{:S(2)}) copy-start(bf16[256,256]{1,0:T(8,128)(2,1)} %wq_ref.3) | copy-start | bytes 393220
  86.7 7.5 %copy-start.13 = (f32[2,64,256]{2,1,0:T(8,128)S(1)}, f32[2,64,256]{2,1,0:T(8,128)}, u32[]{:S(2)}) copy-start(f32[2,64,256]{2,1,0:T(8,128)} %copy-done.12) | copy-start | bytes 393220
  86.7 20.1 %all-to-all-start.3 = ((bf16[64,4,128]{2,1,0:T(4,128)(2,1)}), bf16[64,4,128]{2,1,0:T(4,128)(2,1)S(1)}, u32[]{:S(2)}, u32[]{:S(2)}) async-start(bf16[64,4,128]{2,1,0:T(4,128)(2,1)} %bitcast.8), calls=%async_computation.3 | async-start | bytes 131072 | tf_op jit(solution)/shard_map/all_to_all | solution.py:300
  94.3 12.5 %copy-start.14 = (bf16[256,256]{1,0:T(8,128)(2,1)S(1)}, bf16[256,256]{1,0:T(8,128)(2,1)}, u32[]{:S(2)}) copy-start(bf16[256,256]{1,0:T(8,128)(2,1)} %wo_ref.3) | copy-start | bytes 393220
  94.3 3.5 %collective-permute-start.3 = (f32[64,256]{1,0:T(8,128)S(1)}, f32[64,256]{1,0:T(8,128)S(1)}, u32[]{:S(2)}, u32[]{:S(2)}) collective-permute-start(f32[64,256]{1,0:T(8,128)S(1)} %get-tuple-element.17), channel_id=1, source_target_pairs={{0,8},{8,0},{1,9},{9,1},{2,10},{10,2},{3,11},{11,3},{4,12},{12,4},... | collective-permute-start | bytes 196616 | tf_op jit(solution)/shard_map/ppermute | solution.py:287

commit v2 on v1

v2 whole, which is shorter than its diff:
```python
import functools

import jax
import jax.numpy as jnp
from jax import lax
from jax.experimental import pallas as pl
from jax.experimental.pallas import tpu as pltpu
from jax.sharding import Mesh, PartitionSpec as P

EPS = 1e-05
HEADS = 8
HEAD_SIZE = 32
FEATURES = HEADS * HEAD_SIZE
SCALE = HEAD_SIZE ** (-0.5)
Y, ZH, C, ZL, X = 8, 4, 2, 2, 4
SEQ = ("y", "zh", "c")
RES = ("zl", "x")
CHIPS = Y * ZH
BLOCKS = ZL * X
TURN = (4, 3, 1, 5, 7, 2, 0, 6)
TURN_BITS = sum(y << (4 * n) for n, y in enumerate(TURN))
VMEM = pl.BlockSpec(memory_space=pltpu.VMEM)
SMEM = pl.BlockSpec(memory_space=pltpu.SMEM)
HBM = pl.BlockSpec(memory_space=pltpu.HBM)
NT = (((1,), (1,)), ((), ()))
F32, BF16 = jnp.float32, jnp.bfloat16


def call(kernel, out_shape, *args, scratch=(), smem=0, hbm=0, flops=0, size=0, vmem=6):
    vmem_count = len(args) - smem - hbm
    pinned = [pltpu.with_memory_space_constraint(x, pltpu.HBM) for x in args[len(args) - hbm :]]
    return pl.pallas_call(
        kernel,
        out_shape=out_shape,
        in_specs=[SMEM] * smem + [VMEM] * vmem_count + [HBM] * hbm,
        out_specs=jax.tree.map(lambda _: VMEM, out_shape),
        scratch_shapes=list(scratch),
        compiler_params=pltpu.CompilerParams(vmem_limit_bytes=vmem * 2**20),
        cost_estimate=pl.CostEstimate(flops=flops, bytes_accessed=size, transcendentals=0),
    )(*args[: len(args) - hbm], *pinned)


def standardize(rows):
    centre = jnp.mean(rows, axis=-1, keepdims=True)
    moved = rows - centre
    spread = jnp.mean(moved * moved, axis=-1, keepdims=True)
    return moved * lax.rsqrt(spread + EPS)


def matmul(a, b):
    return jnp.dot(a, b, preferred_element_type=F32)


def head_mask(shape, head):
    lane = lax.broadcasted_iota(jnp.int32, shape, 1)
    return (lane >= head * HEAD_SIZE) & (lane < (head + 1) * HEAD_SIZE)


def pair_kernel(w_hbm, x_ref, out_ref, w_ref, x_scr, scr, sems):
    count = x_ref.shape[0]
    parts = sems.shape[0] - 1
    step = count // parts
    first = pltpu.make_async_copy(w_hbm, w_ref, sems.at[parts])
    first.start()
    copies = []
    for n in range(parts):
        part = pl.ds(n * step, step)
        copies.append(pltpu.make_async_copy(x_ref.at[part], x_scr.at[part], sems.at[n]))
        copies[n].start()
    first.wait()
    w = w_ref[...]
    wh = w.astype(BF16)
    wl = (w - wh.astype(F32)).astype(BF16)
    top = jnp.concatenate([wh.astype(F32), wh.astype(F32)], axis=1)
    low = jnp.concatenate([wl.astype(F32), jnp.zeros_like(w)], axis=1)
    weights = jnp.concatenate([top, low], axis=0).astype(BF16)
    for i in range(count):
        if i % step == 0:
            copies[i // step].wait()
        d = standardize(x_scr[i])
        dh = d.astype(BF16)
        dl = (d - dh.astype(F32)).astype(BF16)
        both = jnp.concatenate([dh, dl], axis=1)
        part = lax.dot_general(weights, both, NT, preferred_element_type=F32)
        scr[:, i, :] = part[:HEADS] + part[HEADS:]
    out_ref[...] = scr[...].astype(BF16)


def norm_kernel(x_ref, out_ref):
    out_ref[...] = standardize(x_ref[...]).astype(BF16)


def query_kernel(c_ref, rows_ref, wq_ref, wg_ref, q_ref, g_ref, mine_ref):
    core = c_ref[0]
    mine = jnp.concatenate([rows_ref[core, :, core], rows_ref[1 - core, :, core]], axis=0)
    mine = mine.reshape(-1, FEATURES)
    mine_ref[...] = mine.reshape(mine_ref.shape)
    tokens = standardize(mine).astype(BF16)
    g_ref[...] = jax.nn.sigmoid(matmul(tokens, wg_ref[...])).reshape(g_ref.shape)
    q_ref[...] = matmul(tokens, wq_ref[...]).astype(BF16).reshape(q_ref.shape)


def row_kernel(
    c_ref, here_ref, q_ref, own_ref, pair_ref, wk_ref, wv_ref, bias_ref, g_ref, rows_ref, wo_ref,
    mid_ref, pair_mid_ref, send_ref, s_scr, p_scr, v_scr, t_scr
):
    count = rows_ref.shape[1]
    keys = own_ref.shape[0]
    cols = keys // BLOCKS
    here = here_ref[0]
    at = []
    for n in range(BLOCKS):
        block = (n % ZL) * X + n // ZL
        at.append((here ^ ((TURN_BITS >> (4 * (here ^ block))) & 7)) * ZH)
    gated, outs, sums = [], [], []

    def softmax(s):
        for h in range(HEADS):
            lo, hi = h * count, (h + 1) * count
            logits = []
            for n in range(BLOCKS):
                bias = bias_ref[pl.ds(at[n], ZH), h].astype(F32).reshape(count, cols)
                logits.append(s_scr[s, lo:hi, n * cols : (n + 1) * cols] * SCALE + bias)
            top = functools.reduce(jnp.maximum, logits)
            top = jnp.max(top, axis=-1, keepdims=True)
            total = None
            for n in range(BLOCKS):
                e = jnp.exp(logits[n] - top)
                total = e if total is None else total + e
                p_scr[s, lo:hi, n * cols : (n + 1) * cols] = e.astype(BF16)
            sums.append(jnp.sum(total, axis=-1, keepdims=True))

    for s, ref in enumerate((own_ref, pair_ref)):
        tokens = ref[...]
        k = matmul(tokens, wk_ref[...]).astype(BF16)
        v_scr[s] = matmul(tokens, wv_ref[...]).astype(BF16)
        q = q_ref[s].astype(F32)
        masked = [jnp.where(head_mask(q.shape, h), q, 0.0).astype(BF16) for h in range(HEADS)]
        masked = jnp.concatenate(masked, axis=0)
        s_scr[s] = lax.dot_general(masked, k, NT, preferred_element_type=F32)
    for s in range(2):
        softmax(s)
        outs.append(matmul(p_scr[s], v_scr[s]))
    for s in range(2):
        attended = jnp.zeros((count, FEATURES), F32)
        for h in range(HEADS):
            part = outs[s][h * count : (h + 1) * count] / sums[s * HEADS + h]
            attended = jnp.where(head_mask(attended.shape, h), part, attended)
        gated.append((g_ref[s] * attended).astype(BF16))
    delta = matmul(jnp.concatenate(gated, axis=0), wo_ref[...])
    mids = [rows_ref[s] + delta[s * count : (s + 1) * count] for s in range(2)]
    mid_ref[...] = mids[0]
    pair_mid_ref[...] = mids[1]
    normed = [standardize(mid) for mid in mids]
    first = c_ref[0] == 0
    ordered = [jnp.where(first, normed[0], normed[1]), jnp.where(first, normed[1], normed[0])]
    for s in range(2):
        for rr in range(2):
            for half in range(2):
                block = ordered[s][rr * CHIPS : (rr + 1) * CHIPS, half * 128 : (half + 1) * 128]
                t_scr[pl.ds(s * 4 + rr * 2 + half, CHIPS, stride=8), :] = block
    send_ref[...] = t_scr[...].reshape(CHIPS, 8, 128).astype(BF16)


def row_call(core_ref, here_ref, q, own, pair, wk, wv, wide, g, mine, wo):
    half, keys = mine.shape[1], own.shape[0]
    return call(
        row_kernel,
        (
            jax.ShapeDtypeStruct((half, FEATURES), F32),
            jax.ShapeDtypeStruct((half, FEATURES), F32),
            jax.ShapeDtypeStruct((CHIPS, 8, 128), BF16),
        ),
        core_ref,
        here_ref,
        q,
        own,
        pair,
        wk,
        wv,
        wide,
        g,
        mine,
        wo,
        smem=2,
        scratch=[
            pltpu.VMEM((2, HEADS * half, keys), F32),
            pltpu.VMEM((2, HEADS * half, keys), BF16),
            pltpu.VMEM((2, keys, FEATURES), BF16),
            pltpu.VMEM((CHIPS * 8, 128), F32),
        ],
        flops=2 * 2 * 2 * HEADS * half * keys * FEATURES,
        size=6 * 2**20,
        vmem=20,
    )


def column_kernel(x_ref, wq_ref, wk_ref, wv_ref, wg_ref, out_ref, t_scr):
    t_scr[...] = x_ref[...].astype(F32).reshape(CHIPS * 8, 128)
    part = [t_scr[pl.ds(i, CHIPS, stride=8), :] for i in range(8)]
    count = 2 * CHIPS
    tokens = jnp.concatenate(
        [
            jnp.concatenate([part[s * 4 + rr * 2], part[s * 4 + rr * 2 + 1]], axis=1)
            for rr in range(2)
            for s in range(2)
        ],
        axis=0,
    ).astype(BF16)
    q = matmul(tokens, wq_ref[...])
    k = matmul(tokens, wk_ref[...]).astype(BF16)
    v = matmul(tokens, wv_ref[...]).astype(BF16)
    g = jax.nn.sigmoid(matmul(tokens, wg_ref[...]))
    for rr in range(2):
        lo, hi = rr * count, (rr + 1) * count
        masked = jnp.concatenate(
            [jnp.where(head_mask((count, FEATURES), h), q[lo:hi], 0.0) for h in range(HEADS)], axis=0
        ).astype(BF16)
        logits = lax.dot_general(masked, k[lo:hi], NT, preferred_element_type=F32) * SCALE
        e = jnp.exp(logits - jnp.max(logits, axis=-1, keepdims=True))
        total = jnp.sum(e, axis=-1, keepdims=True)
        out = matmul(e.astype(BF16), v[lo:hi]) / total
        attended = jnp.zeros((count, FEATURES), F32)
        for h in range(HEADS):
            attended = jnp.where(
                head_mask(attended.shape, h), out[h * count : (h + 1) * count], attended
            )
        gated = g[lo:hi] * attended
        for s in range(2):
            for half in range(2):
                t_scr[pl.ds(s * 4 + rr * 2 + half, CHIPS, stride=8), :] = gated[
                    s * CHIPS : (s + 1) * CHIPS, half * 128 : (half + 1) * 128
                ]
    out_ref[...] = t_scr[...].reshape(CHIPS, 8, 128).astype(BF16)


def final_kernel(c_ref, x_ref, own_ref, pair_ref, wo_ref, out_ref, t_scr):
    t_scr[...] = x_ref[...].astype(F32).reshape(CHIPS * 8, 128)
    part = [t_scr[pl.ds(i, CHIPS, stride=8), :] for i in range(8)]
    tokens = jnp.concatenate(
        [
            jnp.concatenate([part[s * 4 + rr * 2], part[s * 4 + rr * 2 + 1]], axis=1)
            for s in range(2)
            for rr in range(2)
        ],
        axis=0,
    ).astype(BF16)
    update = matmul(tokens, wo_ref[...])
    first = c_ref[0] == 0
    own, pair = own_ref[...], pair_ref[...]
    middle = [jnp.where(first, own, pair), jnp.where(first, pair, own)]
    count = own.shape[0]
    step = count // ZH
    for s in range(2):
        result = middle[s] + update[s * count : (s + 1) * count]
        for z in range(ZH):
            at = (z * 2 + s) * step
            out_ref[at : at + step] = result[z * step : (z + 1) * step]


def shards(
    alignment,
    pair,
    offset_matrix,
    row_wq,
    row_wk,
    row_wv,
    row_wg,
    row_wo,
    col_wq,
    col_wk,
    col_wv,
    col_wg,
    col_wo,
):
    core = lax.axis_index("c").astype(jnp.int32)
    core_ref = core.reshape(1)
    tokens = alignment.shape[1]
    half = tokens // 2
    swap = [(0, 1), (1, 0)]
    turn = [
        (b * BLOCKS + r, (b ^ TURN[b ^ r]) * BLOCKS + b) for b in range(BLOCKS) for r in range(BLOCKS)
    ]

    pair_shape = pair.shape
    bias_shape = (HEADS, pair_shape[0], pair_shape[1])
    bias_here = call(
        pair_kernel,
        jax.ShapeDtypeStruct(bias_shape, BF16),
        offset_matrix.T,
        pair,
        hbm=2,
        scratch=[
            pltpu.VMEM((HEADS, pair_shape[2]), F32),
            pltpu.VMEM(pair_shape, F32),
            pltpu.VMEM(bias_shape, F32),
            pltpu.SemaphoreType.DMA((2,)),
        ],
    )
    bias = lax.ppermute(bias_here, ("y", "zl", "x"), turn)
    normed = call(norm_kernel, jax.ShapeDtypeStruct((tokens, FEATURES), BF16), alignment[0])
    near_normed = lax.all_gather(normed, "zl", axis=0, tiled=True)
    near_normed, bias = lax.optimization_barrier((near_normed, bias))
    own_normed = lax.all_gather(near_normed, "x", axis=0, tiled=True)
    pair_normed = lax.ppermute(own_normed, "c", swap)
    rows = lax.all_gather(alignment, "c", axis=0, tiled=True)
    rows = rows.reshape(2, ZH, 2, half // ZH, FEATURES)

    wide = jnp.broadcast_to(bias[None], (CHIPS,) + bias.shape)
    wide = lax.all_to_all(wide, ("y", "zh"), 0, 0, tiled=True)

    here_ref = lax.axis_index(RES).astype(jnp.int32).reshape(1)
    q, g, mine = call(
        query_kernel,
        (
            jax.ShapeDtypeStruct((2, half, FEATURES), BF16),
            jax.ShapeDtypeStruct((2, half, FEATURES), F32),
            jax.ShapeDtypeStruct((2, half, FEATURES), F32),
        ),
        core_ref,
        rows,
        row_wq,
        row_wg,
        smem=1,
        flops=2 * 2 * half * FEATURES * 2 * FEATURES,
        size=2**20,
    )
    middle, middle_pair, send = row_call(
        core_ref, here_ref, q, own_normed, pair_normed, row_wk, row_wv, wide, g, mine, row_wo
    )
    middle_pair = lax.ppermute(middle_pair, "c", swap)

    block = lax.all_to_all(send, ("y", "zh"), 0, 0, tiled=True)
    gated = call(
        column_kernel,
        jax.ShapeDtypeStruct((CHIPS, 8, 128), BF16),
        block,
        col_wq,
        col_wk,
        col_wv,
        col_wg,
        scratch=[pltpu.VMEM((CHIPS * 8, 128), F32)],
    )
    back = lax.all_to_all(gated.reshape(2 * CHIPS, 4, 128), SEQ, 0, 0, tiled=True)
    out = call(
        final_kernel,
        jax.ShapeDtypeStruct((tokens, FEATURES), F32),
        core_ref,
        back.reshape(CHIPS, 8, 128),
        middle,
        middle_pair,
        col_wo,
        smem=1,
        scratch=[pltpu.VMEM((CHIPS * 8, 128), F32)],
    )
    return out[None]


def solution(mesh):
    fine = Mesh(mesh.devices.reshape(Y, ZH, C, ZL, X), ("y", "zh", "c", "zl", "x"))
    split = P(SEQ, RES, None)
    in_specs = (split, split) + (P(),) * 11
    return jax.shard_map(shards, mesh=fine, in_specs=in_specs, out_specs=split, check_vma=False)
```

time: 108 us -> 101 us (0.935)
  blocking collectives: 19.4 us -> 36.2 us
  waiting for transfers between devices: 28.3 us -> 15.3 us
  local copies, waits for them, and re-layouts: 10.2 us -> 1.27 us
  starting transfers between devices: 42.1 us -> 39.3 us
    all_gather x0 -> x3, blocking collectives: none -> 16.3 us  [the longest x1 10.3 us: shards(): own_normed = lax.all_gather(near_normed, 'x', axis=0, tiled=True)]
    unnamed x44 -> x22, local copies, waits for them, and re-layouts: 8.96 us -> 0.06 us
    all_to_all x1 -> x0, starting transfers between devices: 6.79 us -> none  [shards(): lax.all_to_all(spread, RES, 0, 0, tiled=True).reshape(8 * tokens, FEATURES)]
    all_to_all x1, waiting for transfers between devices: 11.7 us -> 5.27 us  [shards(): wide = lax.all_to_all(wide, ('y', 'zh'), 0, 0, tiled=True)]
    all_to_all x1 -> x0, waiting for transfers between devices: 5.52 us -> none  [shards(): lax.all_to_all(spread, RES, 0, 0, tiled=True).reshape(8 * tokens, FEATURES)]
    ppermute x3 -> x2, starting transfers between devices: 5.32 us -> 10.8 us  [the longest x1 8.28 us: shards(): bias = lax.ppermute(bias_here, ('y', 'zl', 'x'), turn)]
    all_to_all x1, starting transfers between devices: 18.2 us -> 13.2 us  [shards(): wide = lax.all_to_all(wide, ('y', 'zh'), 0, 0, tiled=True)]
    ppermute x1, starting transfers between devices: 4.28 us -> 7.26 us  [shards(): pair_normed = lax.ppermute(own_normed, 'c', swap)]
  transfers between devices with their start and end apart: 7 -> 5, of which waited for: 5 -> 3; matrix products, arithmetic and copies ran while one was open for 0% -> 0% of each run, Pallas kernels for 2% -> 1%
where the time goes in v2:
time: 101 us; the launch traced here: 100 us
  starting transfers between devices  39.3 us (39%)
  blocking collectives  36.2 us (36%)
  waiting for transfers between devices  15.3 us (15%)
  Pallas kernels  7.9 us (8%)
  local copies, waits for them, and re-layouts  1.27 us (1%)
    all_to_all x1, blocking collectives, shards(): block = lax.all_to_all(send, ('y', 'zh'), 0, 0, tiled=True)  19.9 us
    all_to_all x1, starting transfers between devices, shards(): wide = lax.all_to_all(wide, ('y', 'zh'), 0, 0, tiled=True)  13.2 us
    all_gather x1, blocking collectives, shards(): own_normed = lax.all_gather(near_normed, 'x', axis=0, tiled=True)  10.3 us
    all_to_all x1, waiting for transfers between devices, shards(): lax.all_to_all(gated.reshape(2 * CHIPS, 4, 128), SEQ, 0, 0, tiled=True)  9.17 us
    ppermute x1, starting transfers between devices, shards(): bias = lax.ppermute(bias_here, ('y', 'zl', 'x'), turn)  8.28 us
    all_to_all x1, starting transfers between devices, shards(): lax.all_to_all(gated.reshape(2 * CHIPS, 4, 128), SEQ, 0, 0, tiled=True)  8.04 us
    pallas_call x6, Pallas kernels, call(): pl.pallas_call(kernel, out_shape=out_shape, in_specs=[SMEM] * smem + [VME...  7.9 us
    ppermute x1, starting transfers between devices, shards(): pair_normed = lax.ppermute(own_normed, 'c', swap)  7.26 us
  transfers between devices with their start and end apart: 5, of which 3 were waited for; matrix products, arithmetic and copies ran while one was open for 0% of the time, Pallas kernels for 1%

profile of v2, /device:TPU:1, one launch (start us, length us, event | category | flops | bytes accessed | tf_op | source)
XLA Modules:
  0.0 100.2 jit_solution(4092014359246063641)
XLA Ops:
  0.0 2.2 %shard_map.129 = bf16[8,16,128]{2,1,0:T(8,128)(2,1)S(1)} custom-call(f32[8,128]{1,0:T(8,128)} %bitcast.11, f32[16,128,128]{2,1,0:T(8,128)} %x_ref.1), custom_call_target="tpu_custom_call" | custom-call | tf_op jit(solution)/shard_map/pallas_call | solution.py:32
  2.2 8.3 %collective-permute-start = (bf16[8,16,128]{2,1,0:T(8,128)(2,1)S(1)}, bf16[8,16,128]{2,1,0:T(8,128)(2,1)S(1)}, u32[]{:S(2)}, u32[]{:S(2)}) collective-permute-start(bf16[8,16,128]{2,1,0:T(8,128)(2,1)S(1)} %shard_map.129), channel_id=1, source_target_pairs={{0,256},{1,192},{2,64},{3,320},{4,448},{5,128},{6,0},{7,384},{64,1... | collective-permute-start | bytes 98312 | tf_op jit(solution)/shard_map/ppermute | solution.py:300
  10.5 0.0 copy-done
  10.5 0.2 shard_map.128
  10.7 3.8 %all_gather.10 = bf16[256,256]{1,0:T(8,128)(2,1)S(1)} all-gather(bf16[128,256]{1,0:T(8,128)(2,1)S(1)} %shard_map.128), channel_id=1, replica_groups=mesh['y'=8,'zh'=4,'c'=2,'zl'=2,'x'=4] {'zl'}, dimensions={0}, use_global_device_ids=true | all-gather | bytes 196608 | tf_op jit(solution)/shard_map/all_gather | solution.py:302
  14.5 0.0 collective-permute-done
  14.5 1.2 %broadcast_in_dim.4 = bf16[32,8,16,128]{3,2,1,0:T(8,128)(2,1)} broadcast(bf16[8,16,128]{2,1,0:T(8,128)(2,1)S(1)} %collective-permute-done), dimensions={1,2,3} | broadcast | bytes 1081344 | tf_op jit(solution)/shard_map/broadcast_in_dim | solution.py:309
  15.7 13.2 %all-to-all-start = ((bf16[32,8,16,128]{3,2,1,0:T(8,128)(2,1)}), bf16[32,8,16,128]{3,2,1,0:T(8,128)(2,1)S(1)}, u32[]{:S(2)}, u32[]{:S(2)}) async-start(bf16[32,8,16,128]{3,2,1,0:T(8,128)(2,1)} %broadcast_in_dim.4), calls=%async_computation | async-start | bytes 2097152 | tf_op jit(solution)/shard_map/all_to_all | solution.py:310
  28.9 10.3 %all_gather.11.own_ref = bf16[1024,256]{1,0:T(8,128)(2,1)S(1)} all-gather(bf16[256,256]{1,0:T(8,128)(2,1)S(1)} %all_gather.10), channel_id=1, replica_groups=mesh['y'=8,'zh'=4,'c'=2,'zl'=2,'x'=4] {'x'}, dimensions={0}, use_global_device_ids=true | all-gather | bytes 655360 | tf_op jit(solution)/shard_map/all_gather | solution.py:304
  39.3 7.3 %collective-permute-start.1 = (bf16[1024,256]{1,0:T(8,128)(2,1)S(1)}, bf16[1024,256]{1,0:T(8,128)(2,1)S(1)}, u32[]{:S(2)}, u32[]{:S(2)}) collective-permute-start(bf16[1024,256]{1,0:T(8,128)(2,1)S(1)} %all_gather.11.own_ref), channel_id=1, source_target_pairs={{0,8},{8,0},{1,9},{9,1},{2,10},{10,2},{3,11},{11,3},{4,12},{12,4},... | collective-permute-start | bytes 1572872 | tf_op jit(solution)/shard_map/ppermute | solution.py:305
  46.6 0.0 copy-start.1
  46.6 0.0 copy-start.2
  46.6 2.1 %all_gather.9 = f32[2,128,256]{2,1,0:T(8,128)S(1)} all-gather(f32[1,128,256]{2,1,0:T(8,128)S(1)} %copy-done), channel_id=1, replica_groups=mesh['y'=8,'zh'=4,'c'=2,'zl'=2,'x'=4] {'c'}, dimensions={0}, use_global_device_ids=true | all-gather | bytes 393216 | tf_op jit(solution)/shard_map/all_gather | solution.py:306
  48.7 0.0 copy-start.10
  48.7 0.3 shard_map.127
  49.1 0.0 collective-permute-done.1.pair_ref
  49.1 5.3 %all-to-all-done.bias_ref = bf16[32,8,16,128]{3,2,1,0:T(8,128)(2,1)S(1)} async-done(((bf16[32,8,16,128]{3,2,1,0:T(8,128)(2,1)}), bf16[32,8,16,128]{3,2,1,0:T(8,128)(2,1)S(1)}, u32[]{:S(2)}, u32[]{:S(2)}) %all-to-all-start) | async-done | bytes 1048608 | tf_op jit(solution)/shard_map/all_to_all | solution.py:310
  54.4 0.0 copy-start.4
  54.4 0.0 copy-start.5
  54.4 0.0 copy-start.6
  54.4 2.9 %shard_map.130 = (f32[64,256]{1,0:T(8,128)S(1)}, f32[64,256]{1,0:T(8,128)S(1)}, bf16[32,8,128]{2,1,0:T(8,128)(2,1)S(1)}) custom-call(s32[1]{0:T(128)} %bitcast.c_ref, s32[1]{0:T(128)} %bitcast.1.here_ref, bf16[2,64,256]{2,1,0:T(8,128)(2,1)S(1)} %get-tuple-element.13.q_ref, bf16[1024,256]{1,0:T(8,128)(2,1)S(1)} %all_gather.11.own_ref, ...), custom_call_target="tpu_custom_call" | custom-call | flops 1073741824 | bytes 6291456 | tf_op jit(solution)/shard_map/pallas_call | solution.py:32
  57.3 0.0 copy-start.3
  57.4 19.9 %all_to_all.15.x_ref = bf16[32,8,128]{2,1,0:T(8,128)(2,1)S(1)} all-to-all(bf16[32,8,128]{2,1,0:T(8,128)(2,1)S(1)} %get-tuple-element.18), channel_id=1, replica_groups=mesh['y'=8,'zh'=4,'c'=2,'zl'=2,'x'=4] {'y','zh'}, dimensions={0} | all-to-all | bytes 131072 | tf_op jit(solution)/shard_map/all_to_all | solution.py:333
  77.3 0.0 copy-done.6
  77.3 0.0 copy-done.3
  77.3 1.4 %shard_map.131 = bf16[32,8,128]{2,1,0:T(8,128)(2,1)} custom-call(bf16[32,8,128]{2,1,0:T(8,128)(2,1)S(1)} %all_to_all.15.x_ref, bf16[256,256]{1,0:T(8,128)(2,1)S(1)} %copy-done.3, bf16[256,256]{1,0:T(8,128)(2,1)S(1)} %copy-done.4, bf16[256,256]{1,0:T(8,128)(2,1)S(1)} %copy-done.5, bf16[256,256]{1,0:T(8,128)(2,1)S(1)} %copy-done.6), custom_call_target="tpu_custom_call" | custom-call | tf_op jit(solution)/shard_map/pallas_call | solution.py:32
  78.8 8.0 %all-to-all-start.2 = ((bf16[64,4,128]{2,1,0:T(4,128)(2,1)}), bf16[64,4,128]{2,1,0:T(4,128)(2,1)S(1)}, u32[]{:S(2)}, u32[]{:S(2)}) async-start(bf16[64,4,128]{2,1,0:T(4,128)(2,1)} %bitcast.5), calls=%async_computation.2 | async-start | bytes 131072 | tf_op jit(solution)/shard_map/all_to_all | solution.py:344
  86.8 2.5 %collective-permute-start.2 = (f32[64,256]{1,0:T(8,128)S(1)}, f32[64,256]{1,0:T(8,128)S(1)}, u32[]{:S(2)}, u32[]{:S(2)}) collective-permute-start(f32[64,256]{1,0:T(8,128)S(1)} %get-tuple-element.20), channel_id=1, source_target_pairs={{0,8},{8,0},{1,9},{9,1},{2,10},{10,2},{3,11},{11,3},{4,12},{12,4},... | collective-permute-start | bytes 196616 | tf_op jit(solution)/shard_map/ppermute | solution.py:331
  89.3 0.9 collective-permute-done.2.pair_ref
  90.2 9.2 %all-to-all-done.2 = bf16[64,4,128]{2,1,0:T(4,128)(2,1)S(1)} async-done(((bf16[64,4,128]{2,1,0:T(4,128)(2,1)}), bf16[64,4,128]{2,1,0:T(4,128)(2,1)S(1)}, u32[]{:S(2)}, u32[]{:S(2)}) %all-to-all-start.2) | async-done | bytes 65568 | tf_op jit(solution)/shard_map/all_to_all | solution.py:344
  99.3 0.0 copy-done.7
  99.3 0.8 shard_map.132
  (11 shorter events, 0.0 us)
Async XLA Ops:
  0.0 10.5 %copy-start = (f32[1,128,256]{2,1,0:T(8,128)S(1)}, f32[1,128,256]{2,1,0:T(8,128)}, u32[]{:S(2)}) copy-start(f32[1,128,256]{2,1,0:T(8,128)} %param.13) | copy-start | bytes 393220
  2.2 12.3 %collective-permute-start = (bf16[8,16,128]{2,1,0:T(8,128)(2,1)S(1)}, bf16[8,16,128]{2,1,0:T(8,128)(2,1)S(1)}, u32[]{:S(2)}, u32[]{:S(2)}) collective-permute-start(bf16[8,16,128]{2,1,0:T(8,128)(2,1)S(1)} %shard_map.129), channel_id=1, source_target_pairs={{0,256},{1,192},{2,64},{3,320},{4,448},{5,128},{6,0},{7,384},{64,1... | collective-permute-start | bytes 98312 | tf_op jit(solution)/shard_map/ppermute | solution.py:300
  15.7 38.7 %all-to-all-start = ((bf16[32,8,16,128]{3,2,1,0:T(8,128)(2,1)}), bf16[32,8,16,128]{3,2,1,0:T(8,128)(2,1)S(1)}, u32[]{:S(2)}, u32[]{:S(2)}) async-start(bf16[32,8,16,128]{3,2,1,0:T(8,128)(2,1)} %broadcast_in_dim.4), calls=%async_computation | async-start | bytes 2097152 | tf_op jit(solution)/shard_map/all_to_all | solution.py:310
  39.3 9.8 %collective-permute-start.1 = (bf16[1024,256]{1,0:T(8,128)(2,1)S(1)}, bf16[1024,256]{1,0:T(8,128)(2,1)S(1)}, u32[]{:S(2)}, u32[]{:S(2)}) collective-permute-start(bf16[1024,256]{1,0:T(8,128)(2,1)S(1)} %all_gather.11.own_ref), channel_id=1, source_target_pairs={{0,8},{8,0},{1,9},{9,1},{2,10},{10,2},{3,11},{11,3},{4,12},{12,4},... | collective-permute-start | bytes 1572872 | tf_op jit(solution)/shard_map/ppermute | solution.py:305
  46.6 2.2 %copy-start.1 = (bf16[256,256]{1,0:T(8,128)(2,1)S(1)}, bf16[256,256]{1,0:T(8,128)(2,1)}, u32[]{:S(2)}) copy-start(bf16[256,256]{1,0:T(8,128)(2,1)} %wq_ref.2) | copy-start | bytes 393220
  46.6 2.1 %copy-start.2 = (bf16[256,256]{1,0:T(8,128)(2,1)S(1)}, bf16[256,256]{1,0:T(8,128)(2,1)}, u32[]{:S(2)}) copy-start(bf16[256,256]{1,0:T(8,128)(2,1)} %wg_ref.2) | copy-start | bytes 393220
  48.7 5.6 %copy-start.8 = (bf16[256,256]{1,0:T(8,128)(2,1)S(1)}, bf16[256,256]{1,0:T(8,128)(2,1)}, u32[]{:S(2)}) copy-start(bf16[256,256]{1,0:T(8,128)(2,1)} %wk_ref.2) | copy-start | bytes 393220
  48.7 5.6 %copy-start.9 = (bf16[256,256]{1,0:T(8,128)(2,1)S(1)}, bf16[256,256]{1,0:T(8,128)(2,1)}, u32[]{:S(2)}) copy-start(bf16[256,256]{1,0:T(8,128)(2,1)} %wv_ref.2) | copy-start | bytes 393220
  48.7 5.6 %copy-start.10 = (bf16[256,256]{1,0:T(8,128)(2,1)S(1)}, bf16[256,256]{1,0:T(8,128)(2,1)}, u32[]{:S(2)}) copy-start(bf16[256,256]{1,0:T(8,128)(2,1)} %wo_ref.2) | copy-start | bytes 393220
  54.4 22.9 %copy-start.4 = (bf16[256,256]{1,0:T(8,128)(2,1)S(1)}, bf16[256,256]{1,0:T(8,128)(2,1)}, u32[]{:S(2)}) copy-start(bf16[256,256]{1,0:T(8,128)(2,1)} %wk_ref.3) | copy-start | bytes 393220
  54.4 22.9 %copy-start.5 = (bf16[256,256]{1,0:T(8,128)(2,1)S(1)}, bf16[256,256]{1,0:T(8,128)(2,1)}, u32[]{:S(2)}) copy-start(bf16[256,256]{1,0:T(8,128)(2,1)} %wv_ref.3) | copy-start | bytes 393220
  54.4 22.9 %copy-start.6 = (bf16[256,256]{1,0:T(8,128)(2,1)S(1)}, bf16[256,256]{1,0:T(8,128)(2,1)}, u32[]{:S(2)}) copy-start(bf16[256,256]{1,0:T(8,128)(2,1)} %wg_ref.3) | copy-start | bytes 393220
  57.3 20.0 %copy-start.3 = (bf16[256,256]{1,0:T(8,128)(2,1)S(1)}, bf16[256,256]{1,0:T(8,128)(2,1)}, u32[]{:S(2)}) copy-start(bf16[256,256]{1,0:T(8,128)(2,1)} %wq_ref.3) | copy-start | bytes 393220
  78.8 20.6 %copy-start.7 = (bf16[256,256]{1,0:T(8,128)(2,1)S(1)}, bf16[256,256]{1,0:T(8,128)(2,1)}, u32[]{:S(2)}) copy-start(bf16[256,256]{1,0:T(8,128)(2,1)} %wo_ref.3) | copy-start | bytes 393220
  78.8 20.6 %all-to-all-start.2 = ((bf16[64,4,128]{2,1,0:T(4,128)(2,1)}), bf16[64,4,128]{2,1,0:T(4,128)(2,1)S(1)}, u32[]{:S(2)}, u32[]{:S(2)}) async-start(bf16[64,4,128]{2,1,0:T(4,128)(2,1)} %bitcast.5), calls=%async_computation.2 | async-start | bytes 131072 | tf_op jit(solution)/shard_map/all_to_all | solution.py:344
  86.8 3.4 %collective-permute-start.2 = (f32[64,256]{1,0:T(8,128)S(1)}, f32[64,256]{1,0:T(8,128)S(1)}, u32[]{:S(2)}, u32[]{:S(2)}) collective-permute-start(f32[64,256]{1,0:T(8,128)S(1)} %get-tuple-element.20), channel_id=1, source_target_pairs={{0,8},{8,0},{1,9},{9,1},{2,10},{10,2},{3,11},{11,3},{4,12},{12,4},... | collective-permute-start | bytes 196616 | tf_op jit(solution)/shard_map/ppermute | solution.py:331

commit v3 on v2

--- a/solution.py
+++ b/solution.py
@@ -102,7 +102,7 @@
 
 def row_kernel(
     c_ref, here_ref, q_ref, own_ref, pair_ref, wk_ref, wv_ref, bias_ref, g_ref, rows_ref, wo_ref,
-    mid_ref, pair_mid_ref, send_ref, s_scr, p_scr, v_scr, t_scr
+    send_ref, s_scr, p_scr, v_scr, t_scr
 ):
     count = rows_ref.shape[1]
     keys = own_ref.shape[0]
@@ -112,7 +112,7 @@
     for n in range(BLOCKS):
         block = (n % ZL) * X + n // ZL
         at.append((here ^ ((TURN_BITS >> (4 * (here ^ block))) & 7)) * ZH)
-    gated, outs, sums = [], [], []
+    gated, outs, shares = [], [], []
 
     def softmax(s):
         for h in range(HEADS):
@@ -128,7 +128,7 @@
                 e = jnp.exp(logits[n] - top)
                 total = e if total is None else total + e
                 p_scr[s, lo:hi, n * cols : (n + 1) * cols] = e.astype(BF16)
-            sums.append(jnp.sum(total, axis=-1, keepdims=True))
+            shares.append(1.0 / jnp.sum(total, axis=-1, keepdims=True))
 
     for s, ref in enumerate((own_ref, pair_ref)):
         tokens = ref[...]
@@ -144,33 +144,28 @@
     for s in range(2):
         attended = jnp.zeros((count, FEATURES), F32)
         for h in range(HEADS):
-            part = outs[s][h * count : (h + 1) * count] / sums[s * HEADS + h]
+            part = outs[s][h * count : (h + 1) * count] * shares[s * HEADS + h]
             attended = jnp.where(head_mask(attended.shape, h), part, attended)
         gated.append((g_ref[s] * attended).astype(BF16))
     delta = matmul(jnp.concatenate(gated, axis=0), wo_ref[...])
-    mids = [rows_ref[s] + delta[s * count : (s + 1) * count] for s in range(2)]
-    mid_ref[...] = mids[0]
-    pair_mid_ref[...] = mids[1]
-    normed = [standardize(mid) for mid in mids]
     first = c_ref[0] == 0
-    ordered = [jnp.where(first, normed[0], normed[1]), jnp.where(first, normed[1], normed[0])]
-    for s in range(2):
-        for rr in range(2):
-            for half in range(2):
-                block = ordered[s][rr * CHIPS : (rr + 1) * CHIPS, half * 128 : (half + 1) * 128]
-                t_scr[pl.ds(s * 4 + rr * 2 + half, CHIPS, stride=8), :] = block
-    send_ref[...] = t_scr[...].reshape(CHIPS, 8, 128).astype(BF16)
+    deltas = [delta[s * count : (s + 1) * count] for s in range(2)]
+    normed = [standardize(rows_ref[s] + deltas[s]) for s in range(2)]
+    for kind, (own, pair) in enumerate((normed, deltas)):
+        ordered = [jnp.where(first, own, pair), jnp.where(first, pair, own)]
+        for s in range(2):
+            for rr in range(2):
+                for half in range(2):
+                    block = ordered[s][rr * CHIPS : (rr + 1) * CHIPS, half * 128 : (half + 1) * 128]
+                    t_scr[pl.ds(kind * 8 + s * 4 + rr * 2 + half, CHIPS, stride=16), :] = block
+    send_ref[...] = t_scr[...].reshape(CHIPS, 16, 128).astype(BF16)
 
 
 def row_call(core_ref, here_ref, q, own, pair, wk, wv, wide, g, mine, wo):
     half, keys = mine.shape[1], own.shape[0]
     return call(
         row_kernel,
-        (
-            jax.ShapeDtypeStruct((half, FEATURES), F32),
-            jax.ShapeDtypeStruct((half, FEATURES), F32),
-            jax.ShapeDtypeStruct((CHIPS, 8, 128), BF16),
-        ),
+        jax.ShapeDtypeStruct((CHIPS, 16, 128), BF16),
         core_ref,
         here_ref,
         q,
@@ -187,7 +182,7 @@
             pltpu.VMEM((2, HEADS * half, keys), F32),
             pltpu.VMEM((2, HEADS * half, keys), BF16),
             pltpu.VMEM((2, keys, FEATURES), BF16),
-            pltpu.VMEM((CHIPS * 8, 128), F32),
+            pltpu.VMEM((CHIPS * 16, 128), F32),
         ],
         flops=2 * 2 * 2 * HEADS * half * keys * FEATURES,
         size=6 * 2**20,
@@ -195,22 +190,25 @@
     )
 
 
-def column_kernel(x_ref, wq_ref, wk_ref, wv_ref, wg_ref, out_ref, t_scr):
-    t_scr[...] = x_ref[...].astype(F32).reshape(CHIPS * 8, 128)
-    part = [t_scr[pl.ds(i, CHIPS, stride=8), :] for i in range(8)]
+def column_kernel(x_ref, wq_ref, wk_ref, wv_ref, wg_ref, wo_ref, out_ref, t_scr, u_scr):
+    t_scr[...] = x_ref[...].astype(F32).reshape(CHIPS * 16, 128)
+    part = [t_scr[pl.ds(i, CHIPS, stride=16), :] for i in range(16)]
     count = 2 * CHIPS
-    tokens = jnp.concatenate(
-        [
-            jnp.concatenate([part[s * 4 + rr * 2], part[s * 4 + rr * 2 + 1]], axis=1)
+
+    def tokens_of(kind):
+        rows = [
+            jnp.concatenate([part[kind * 8 + s * 4 + rr * 2], part[kind * 8 + s * 4 + rr * 2 + 1]], axis=1)
             for rr in range(2)
             for s in range(2)
-        ],
-        axis=0,
-    ).astype(BF16)
+        ]
+        return jnp.concatenate(rows, axis=0)
+
+    tokens = tokens_of(0).astype(BF16)
     q = matmul(tokens, wq_ref[...])
     k = matmul(tokens, wk_ref[...]).astype(BF16)
     v = matmul(tokens, wv_ref[...]).astype(BF16)
     g = jax.nn.sigmoid(matmul(tokens, wg_ref[...]))
+    gated = []
     for rr in range(2):
         lo, hi = rr * count, (rr + 1) * count
         masked = jnp.concatenate(
@@ -218,44 +216,37 @@
         ).astype(BF16)
         logits = lax.dot_general(masked, k[lo:hi], NT, preferred_element_type=F32) * SCALE
         e = jnp.exp(logits - jnp.max(logits, axis=-1, keepdims=True))
-        total = jnp.sum(e, axis=-1, keepdims=True)
-        out = matmul(e.astype(BF16), v[lo:hi]) / total
+        share = 1.0 / jnp.sum(e, axis=-1, keepdims=True)
+        out = matmul(e.astype(BF16), v[lo:hi]) * share
         attended = jnp.zeros((count, FEATURES), F32)
         for h in range(HEADS):
             attended = jnp.where(
                 head_mask(attended.shape, h), out[h * count : (h + 1) * count], attended
             )
-        gated = g[lo:hi] * attended
+        gated.append((g[lo:hi] * attended).astype(BF16))
+    update = tokens_of(1) + matmul(jnp.concatenate(gated, axis=0), wo_ref[...])
+    for rr in range(2):
         for s in range(2):
+            at = (rr * 2 + s) * CHIPS
             for half in range(2):
-                t_scr[pl.ds(s * 4 + rr * 2 + half, CHIPS, stride=8), :] = gated[
-                    s * CHIPS : (s + 1) * CHIPS, half * 128 : (half + 1) * 128
+                u_scr[pl.ds(s * CHIPS * 4 + rr * 2 + half, CHIPS, stride=4), :] = update[
+                    at : at + CHIPS, half * 128 : (half + 1) * 128
                 ]
-    out_ref[...] = t_scr[...].reshape(CHIPS, 8, 128).astype(BF16)
-
-
-def final_kernel(c_ref, x_ref, own_ref, pair_ref, wo_ref, out_ref, t_scr):
-    t_scr[...] = x_ref[...].astype(F32).reshape(CHIPS * 8, 128)
-    part = [t_scr[pl.ds(i, CHIPS, stride=8), :] for i in range(8)]
-    tokens = jnp.concatenate(
-        [
-            jnp.concatenate([part[s * 4 + rr * 2], part[s * 4 + rr * 2 + 1]], axis=1)
-            for s in range(2)
-            for rr in range(2)
-        ],
-        axis=0,
-    ).astype(BF16)
-    update = matmul(tokens, wo_ref[...])
-    first = c_ref[0] == 0
-    own, pair = own_ref[...], pair_ref[...]
-    middle = [jnp.where(first, own, pair), jnp.where(first, pair, own)]
-    count = own.shape[0]
-    step = count // ZH
+    out_ref[...] = u_scr[...].astype(BF16)
+
+
+def final_kernel(x_ref, rows_ref, out_ref, t_scr):
+    t_scr[...] = x_ref[...].astype(F32)
+    part = [t_scr[pl.ds(s * CHIPS * 4 + i, CHIPS, stride=4), :] for s in range(2) for i in range(4)]
+    step = rows_ref.shape[0] // (2 * ZH)
     for s in range(2):
-        result = middle[s] + update[s * count : (s + 1) * count]
+        update = jnp.concatenate(
+            [jnp.concatenate([part[s * 4 + rr * 2], part[s * 4 + rr * 2 + 1]], axis=1) for rr in range(2)],
+            axis=0,
+        )
         for z in range(ZH):
             at = (z * 2 + s) * step
-            out_ref[at : at + step] = result[z * step : (z + 1) * step]
+            out_ref[at : at + step] = rows_ref[at : at + step] + update[z * step : (z + 1) * step]
 
 
 def shards(
@@ -325,32 +316,28 @@
         flops=2 * 2 * half * FEATURES * 2 * FEATURES,
         size=2**20,
     )
-    middle, middle_pair, send = row_call(
+    send = row_call(
         core_ref, here_ref, q, own_normed, pair_normed, row_wk, row_wv, wide, g, mine, row_wo
     )
-    middle_pair = lax.ppermute(middle_pair, "c", swap)
-
-    block = lax.all_to_all(send, ("y", "zh"), 0, 0, tiled=True)
-    gated = call(
+
+    block = lax.all_to_all(send, ("zh", "y"), 0, 0, tiled=True)
+    update = call(
         column_kernel,
-        jax.ShapeDtypeStruct((CHIPS, 8, 128), BF16),
+        jax.ShapeDtypeStruct((CHIPS * 8, 128), BF16),
         block,
         col_wq,
         col_wk,
         col_wv,
         col_wg,
-        scratch=[pltpu.VMEM((CHIPS * 8, 128), F32)],
-    )
-    back = lax.all_to_all(gated.reshape(2 * CHIPS, 4, 128), SEQ, 0, 0, tiled=True)
+        col_wo,
+        scratch=[pltpu.VMEM((CHIPS * 16, 128), F32), pltpu.VMEM((CHIPS * 8, 128), F32)],
+    )
+    back = lax.all_to_all(update.reshape(2 * CHIPS, 4, 128), ("c", "zh", "y"), 0, 0, tiled=True)
     out = call(
         final_kernel,
         jax.ShapeDtypeStruct((tokens, FEATURES), F32),
-        core_ref,
-        back.reshape(CHIPS, 8, 128),
-        middle,
-        middle_pair,
-        col_wo,
-        smem=1,
+        back.reshape(CHIPS * 8, 128),
+        alignment[0],
         scratch=[pltpu.VMEM((CHIPS * 8, 128), F32)],
     )
     return out[None]

time: 101 us -> 99.4 us (0.984)
  blocking collectives: 36.2 us -> 55.9 us
  starting transfers between devices: 39.3 us -> 28.8 us
  waiting for transfers between devices: 15.3 us -> 5.27 us
    all_to_all x1 -> x2, blocking collectives: 19.9 us -> 39.7 us  [the longest x1 20.4 us: shards(): block = lax.all_to_all(send, ('zh', 'y'), 0, 0, tiled=True)]
    all_to_all x1 -> x0, waiting for transfers between devices: 9.17 us -> none  [shards(): lax.all_to_all(gated.reshape(2 * CHIPS, 4, 128), SEQ, 0, 0, tiled=True)]
    all_to_all x1 -> x0, starting transfers between devices: 8.04 us -> none  [shards(): lax.all_to_all(gated.reshape(2 * CHIPS, 4, 128), SEQ, 0, 0, tiled=True)]
    ppermute x1 -> x0, starting transfers between devices: 2.48 us -> none  [shards(): middle_pair = lax.ppermute(middle_pair, 'c', swap)]
  transfers between devices with their start and end apart: 5 -> 3, of which waited for: 3 -> 1; matrix products, arithmetic and copies ran while one was open for 0% -> 0% of each run, Pallas kernels for 1% -> 1%
where the time goes in v3:
time: 99.4 us; the launch traced here: 98.7 us
  blocking collectives  55.9 us (56%)
  starting transfers between devices  28.8 us (29%)
  Pallas kernels  7.25 us (7%)
  waiting for transfers between devices  5.27 us (5%)
  local copies, waits for them, and re-layouts  1.28 us (1%)
    all_to_all x1, blocking collectives, shards(): block = lax.all_to_all(send, ('zh', 'y'), 0, 0, tiled=True)  20.4 us
    all_to_all x1, blocking collectives, shards(): lax.all_to_all(update.reshape(2 * CHIPS, 4, 128), ('c', 'zh', 'y'), 0, 0,...  19.3 us
    all_to_all x1, starting transfers between devices, shards(): wide = lax.all_to_all(wide, ('y', 'zh'), 0, 0, tiled=True)  13.2 us
    all_gather x1, blocking collectives, shards(): own_normed = lax.all_gather(near_normed, 'x', axis=0, tiled=True)  10.3 us
    ppermute x1, starting transfers between devices, shards(): bias = lax.ppermute(bias_here, ('y', 'zl', 'x'), turn)  8.28 us
    ppermute x1, starting transfers between devices, shards(): pair_normed = lax.ppermute(own_normed, 'c', swap)  7.26 us
    pallas_call x6, Pallas kernels, call(): pl.pallas_call(kernel, out_shape=out_shape, in_specs=[SMEM] * smem + [VME...  7.25 us
    all_to_all x1, waiting for transfers between devices, shards(): wide = lax.all_to_all(wide, ('y', 'zh'), 0, 0, tiled=True)  5.27 us
  transfers between devices with their start and end apart: 3, of which 1 were waited for; matrix products, arithmetic and copies ran while one was open for 0% of the time, Pallas kernels for 1%

profile of v3, /device:TPU:1, one launch (start us, length us, event | category | flops | bytes accessed | tf_op | source)
XLA Modules:
  0.0 98.7 jit_solution(15701898630907184325)
XLA Ops:
  0.0 2.2 %shard_map.129 = bf16[8,16,128]{2,1,0:T(8,128)(2,1)S(1)} custom-call(f32[8,128]{1,0:T(8,128)} %bitcast.13, f32[16,128,128]{2,1,0:T(8,128)} %x_ref.1), custom_call_target="tpu_custom_call" | custom-call | tf_op jit(solution)/shard_map/pallas_call | solution.py:32
  2.2 8.3 %collective-permute-start = (bf16[8,16,128]{2,1,0:T(8,128)(2,1)S(1)}, bf16[8,16,128]{2,1,0:T(8,128)(2,1)S(1)}, u32[]{:S(2)}, u32[]{:S(2)}) collective-permute-start(bf16[8,16,128]{2,1,0:T(8,128)(2,1)S(1)} %shard_map.129), channel_id=1, source_target_pairs={{0,256},{1,192},{2,64},{3,320},{4,448},{5,128},{6,0},{7,384},{64,1... | collective-permute-start | bytes 98312 | tf_op jit(solution)/shard_map/ppermute | solution.py:291
  10.5 0.0 copy-done
  10.5 0.2 shard_map.128
  10.7 3.8 %all_gather.10 = bf16[256,256]{1,0:T(8,128)(2,1)S(1)} all-gather(bf16[128,256]{1,0:T(8,128)(2,1)S(1)} %shard_map.128), channel_id=1, replica_groups=mesh['y'=8,'zh'=4,'c'=2,'zl'=2,'x'=4] {'zl'}, dimensions={0}, use_global_device_ids=true | all-gather | bytes 196608 | tf_op jit(solution)/shard_map/all_gather | solution.py:293
  14.5 0.0 collective-permute-done
  14.5 1.2 %broadcast_in_dim.4 = bf16[32,8,16,128]{3,2,1,0:T(8,128)(2,1)} broadcast(bf16[8,16,128]{2,1,0:T(8,128)(2,1)S(1)} %collective-permute-done), dimensions={1,2,3} | broadcast | bytes 1081344 | tf_op jit(solution)/shard_map/broadcast_in_dim | solution.py:300
  15.7 13.2 %all-to-all-start = ((bf16[32,8,16,128]{3,2,1,0:T(8,128)(2,1)}), bf16[32,8,16,128]{3,2,1,0:T(8,128)(2,1)S(1)}, u32[]{:S(2)}, u32[]{:S(2)}) async-start(bf16[32,8,16,128]{3,2,1,0:T(8,128)(2,1)} %broadcast_in_dim.4), calls=%async_computation | async-start | bytes 2097152 | tf_op jit(solution)/shard_map/all_to_all | solution.py:301
  28.9 10.3 %all_gather.11.own_ref = bf16[1024,256]{1,0:T(8,128)(2,1)S(1)} all-gather(bf16[256,256]{1,0:T(8,128)(2,1)S(1)} %all_gather.10), channel_id=1, replica_groups=mesh['y'=8,'zh'=4,'c'=2,'zl'=2,'x'=4] {'x'}, dimensions={0}, use_global_device_ids=true | all-gather | bytes 655360 | tf_op jit(solution)/shard_map/all_gather | solution.py:295
  39.3 7.3 %collective-permute-start.1 = (bf16[1024,256]{1,0:T(8,128)(2,1)S(1)}, bf16[1024,256]{1,0:T(8,128)(2,1)S(1)}, u32[]{:S(2)}, u32[]{:S(2)}) collective-permute-start(bf16[1024,256]{1,0:T(8,128)(2,1)S(1)} %all_gather.11.own_ref), channel_id=1, source_target_pairs={{0,8},{8,0},{1,9},{9,1},{2,10},{10,2},{3,11},{11,3},{4,12},{12,4},... | collective-permute-start | bytes 1572872 | tf_op jit(solution)/shard_map/ppermute | solution.py:296
  46.6 0.0 copy-start.1
  46.6 0.0 copy-start.2
  46.6 2.1 %all_gather.9 = f32[2,128,256]{2,1,0:T(8,128)S(1)} all-gather(f32[1,128,256]{2,1,0:T(8,128)S(1)} %copy-done), channel_id=1, replica_groups=mesh['y'=8,'zh'=4,'c'=2,'zl'=2,'x'=4] {'c'}, dimensions={0}, use_global_device_ids=true | all-gather | bytes 393216 | tf_op jit(solution)/shard_map/all_gather | solution.py:297
  48.7 0.0 copy-done.1
  48.7 0.0 copy-done.2
  48.7 0.0 copy-start.10
  48.7 0.3 shard_map.127
  49.1 0.0 collective-permute-done.1.pair_ref
  49.1 5.3 %all-to-all-done.bias_ref = bf16[32,8,16,128]{3,2,1,0:T(8,128)(2,1)S(1)} async-done(((bf16[32,8,16,128]{3,2,1,0:T(8,128)(2,1)}), bf16[32,8,16,128]{3,2,1,0:T(8,128)(2,1)S(1)}, u32[]{:S(2)}, u32[]{:S(2)}) %all-to-all-start) | async-done | bytes 1048608 | tf_op jit(solution)/shard_map/all_to_all | solution.py:301
  54.4 0.0 copy-done.8
  54.4 0.0 copy-start.5
  54.4 0.0 copy-start.6
  54.4 0.0 copy-start.7
  54.4 3.0 %shard_map.130 = bf16[32,16,128]{2,1,0:T(8,128)(2,1)S(1)} custom-call(s32[1]{0:T(128)} %bitcast.c_ref, s32[1]{0:T(128)} %bitcast.1.here_ref, bf16[2,64,256]{2,1,0:T(8,128)(2,1)S(1)} %get-tuple-element.10.q_ref, bf16[1024,256]{1,0:T(8,128)(2,1)S(1)} %all_gather.11.own_ref, bf16[1024,256]{1,0:T(8,128)(2,1)S(1)} %collective-permute-done.1.pair_ref, ...), custom_call_target="tpu_custom_call" | custom-call | flops 1073741824 | bytes 6291456 | tf_op jit(solution)/shard_map/pallas_call | solution.py:32
  57.4 0.0 copy-start.3
  57.4 0.0 copy-start.4
  57.4 20.4 %all_to_all.15.x_ref = bf16[32,16,128]{2,1,0:T(8,128)(2,1)S(1)} all-to-all(bf16[32,16,128]{2,1,0:T(8,128)(2,1)S(1)} %shard_map.130), channel_id=1, replica_groups=mesh['y'=8,'zh'=4,'c'=2,'zl'=2,'x'=4] {'zh','y'}, dimensions={0} | all-to-all | bytes 262144 | tf_op jit(solution)/shard_map/all_to_all | solution.py:323
  77.8 0.0 copy-done.3
  77.8 0.0 copy-done.4
  77.8 0.9 shard_map.131
  78.7 19.3 %all_to_all.16 = bf16[64,4,128]{2,1,0:T(4,128)(2,1)S(1)} all-to-all(bf16[64,4,128]{2,1,0:T(4,128)(2,1)S(1)} %bitcast.12), channel_id=1, replica_groups=mesh['y'=8,'zh'=4,'c'=2,'zl'=2,'x'=4] {'c','zh','y'}, dimensions={0} | all-to-all | bytes 131072 | tf_op jit(solution)/shard_map/all_to_all | solution.py:335
  98.0 0.7 shard_map.132
  (8 shorter events, 0.0 us)
Async XLA Ops:
  0.0 10.5 %copy-start = (f32[1,128,256]{2,1,0:T(8,128)S(1)}, f32[1,128,256]{2,1,0:T(8,128)}, u32[]{:S(2)}) copy-start(f32[1,128,256]{2,1,0:T(8,128)} %param.13) | copy-start | bytes 393220
  2.2 12.3 %collective-permute-start = (bf16[8,16,128]{2,1,0:T(8,128)(2,1)S(1)}, bf16[8,16,128]{2,1,0:T(8,128)(2,1)S(1)}, u32[]{:S(2)}, u32[]{:S(2)}) collective-permute-start(bf16[8,16,128]{2,1,0:T(8,128)(2,1)S(1)} %shard_map.129), channel_id=1, source_target_pairs={{0,256},{1,192},{2,64},{3,320},{4,448},{5,128},{6,0},{7,384},{64,1... | collective-permute-start | bytes 98312 | tf_op jit(solution)/shard_map/ppermute | solution.py:291
  15.7 38.7 %all-to-all-start = ((bf16[32,8,16,128]{3,2,1,0:T(8,128)(2,1)}), bf16[32,8,16,128]{3,2,1,0:T(8,128)(2,1)S(1)}, u32[]{:S(2)}, u32[]{:S(2)}) async-start(bf16[32,8,16,128]{3,2,1,0:T(8,128)(2,1)} %broadcast_in_dim.4), calls=%async_computation | async-start | bytes 2097152 | tf_op jit(solution)/shard_map/all_to_all | solution.py:301
  39.3 9.8 %collective-permute-start.1 = (bf16[1024,256]{1,0:T(8,128)(2,1)S(1)}, bf16[1024,256]{1,0:T(8,128)(2,1)S(1)}, u32[]{:S(2)}, u32[]{:S(2)}) collective-permute-start(bf16[1024,256]{1,0:T(8,128)(2,1)S(1)} %all_gather.11.own_ref), channel_id=1, source_target_pairs={{0,8},{8,0},{1,9},{9,1},{2,10},{10,2},{3,11},{11,3},{4,12},{12,4},... | collective-permute-start | bytes 1572872 | tf_op jit(solution)/shard_map/ppermute | solution.py:296
  46.6 2.2 %copy-start.1 = (bf16[256,256]{1,0:T(8,128)(2,1)S(1)}, bf16[256,256]{1,0:T(8,128)(2,1)}, u32[]{:S(2)}) copy-start(bf16[256,256]{1,0:T(8,128)(2,1)} %wq_ref.2) | copy-start | bytes 393220
  46.6 2.1 %copy-start.2 = (bf16[256,256]{1,0:T(8,128)(2,1)S(1)}, bf16[256,256]{1,0:T(8,128)(2,1)}, u32[]{:S(2)}) copy-start(bf16[256,256]{1,0:T(8,128)(2,1)} %wg_ref.2) | copy-start | bytes 393220
  48.7 5.6 %copy-start.8 = (bf16[256,256]{1,0:T(8,128)(2,1)S(1)}, bf16[256,256]{1,0:T(8,128)(2,1)}, u32[]{:S(2)}) copy-start(bf16[256,256]{1,0:T(8,128)(2,1)} %wk_ref.2) | copy-start | bytes 393220
  48.7 5.6 %copy-start.9 = (bf16[256,256]{1,0:T(8,128)(2,1)S(1)}, bf16[256,256]{1,0:T(8,128)(2,1)}, u32[]{:S(2)}) copy-start(bf16[256,256]{1,0:T(8,128)(2,1)} %wv_ref.2) | copy-start | bytes 393220
  48.7 5.6 %copy-start.10 = (bf16[256,256]{1,0:T(8,128)(2,1)S(1)}, bf16[256,256]{1,0:T(8,128)(2,1)}, u32[]{:S(2)}) copy-start(bf16[256,256]{1,0:T(8,128)(2,1)} %wo_ref.2) | copy-start | bytes 393220
  54.4 23.4 %copy-start.5 = (bf16[256,256]{1,0:T(8,128)(2,1)S(1)}, bf16[256,256]{1,0:T(8,128)(2,1)}, u32[]{:S(2)}) copy-start(bf16[256,256]{1,0:T(8,128)(2,1)} %wv_ref.3) | copy-start | bytes 393220
  54.4 23.4 %copy-start.6 = (bf16[256,256]{1,0:T(8,128)(2,1)S(1)}, bf16[256,256]{1,0:T(8,128)(2,1)}, u32[]{:S(2)}) copy-start(bf16[256,256]{1,0:T(8,128)(2,1)} %wg_ref.3) | copy-start | bytes 393220
  54.4 23.4 %copy-start.7 = (bf16[256,256]{1,0:T(8,128)(2,1)S(1)}, bf16[256,256]{1,0:T(8,128)(2,1)}, u32[]{:S(2)}) copy-start(bf16[256,256]{1,0:T(8,128)(2,1)} %wo_ref.3) | copy-start | bytes 393220
  57.4 20.4 %copy-start.3 = (bf16[256,256]{1,0:T(8,128)(2,1)S(1)}, bf16[256,256]{1,0:T(8,128)(2,1)}, u32[]{:S(2)}) copy-start(bf16[256,256]{1,0:T(8,128)(2,1)} %wq_ref.3) | copy-start | bytes 393220
  57.4 20.4 %copy-start.4 = (bf16[256,256]{1,0:T(8,128)(2,1)S(1)}, bf16[256,256]{1,0:T(8,128)(2,1)}, u32[]{:S(2)}) copy-start(bf16[256,256]{1,0:T(8,128)(2,1)} %wk_ref.3) | copy-start | bytes 393220

commit v4 on v3

--- a/solution.py
+++ b/solution.py
@@ -149,23 +149,21 @@
         gated.append((g_ref[s] * attended).astype(BF16))
     delta = matmul(jnp.concatenate(gated, axis=0), wo_ref[...])
     first = c_ref[0] == 0
-    deltas = [delta[s * count : (s + 1) * count] for s in range(2)]
-    normed = [standardize(rows_ref[s] + deltas[s]) for s in range(2)]
-    for kind, (own, pair) in enumerate((normed, deltas)):
-        ordered = [jnp.where(first, own, pair), jnp.where(first, pair, own)]
-        for s in range(2):
-            for rr in range(2):
-                for half in range(2):
-                    block = ordered[s][rr * CHIPS : (rr + 1) * CHIPS, half * 128 : (half + 1) * 128]
-                    t_scr[pl.ds(kind * 8 + s * 4 + rr * 2 + half, CHIPS, stride=16), :] = block
-    send_ref[...] = t_scr[...].reshape(CHIPS, 16, 128).astype(BF16)
+    own, pair = [rows_ref[s] + delta[s * count : (s + 1) * count] for s in range(2)]
+    ordered = [jnp.where(first, own, pair), jnp.where(first, pair, own)]
+    for s in range(2):
+        for rr in range(2):
+            for half in range(2):
+                block = ordered[s][rr * CHIPS : (rr + 1) * CHIPS, half * 128 : (half + 1) * 128]
+                t_scr[pl.ds(s * 4 + rr * 2 + half, CHIPS, stride=8), :] = block
+    send_ref[...] = t_scr[...].reshape(CHIPS, 8, 128).astype(BF16)
 
 
 def row_call(core_ref, here_ref, q, own, pair, wk, wv, wide, g, mine, wo):
     half, keys = mine.shape[1], own.shape[0]
     return call(
         row_kernel,
-        jax.ShapeDtypeStruct((CHIPS, 16, 128), BF16),
+        jax.ShapeDtypeStruct((CHIPS, 8, 128), BF16),
         core_ref,
         here_ref,
         q,
@@ -182,7 +180,7 @@
             pltpu.VMEM((2, HEADS * half, keys), F32),
             pltpu.VMEM((2, HEADS * half, keys), BF16),
             pltpu.VMEM((2, keys, FEATURES), BF16),
-            pltpu.VMEM((CHIPS * 16, 128), F32),
+            pltpu.VMEM((CHIPS * 8, 128), F32),
         ],
         flops=2 * 2 * 2 * HEADS * half * keys * FEATURES,
         size=6 * 2**20,
@@ -190,20 +188,17 @@
     )
 
 
-def column_kernel(x_ref, wq_ref, wk_ref, wv_ref, wg_ref, wo_ref, out_ref, t_scr, u_scr):
-    t_scr[...] = x_ref[...].astype(F32).reshape(CHIPS * 16, 128)
-    part = [t_scr[pl.ds(i, CHIPS, stride=16), :] for i in range(16)]
+def column_kernel(x_ref, wq_ref, wk_ref, wv_ref, wg_ref, wo_ref, out_ref, t_scr):
+    t_scr[...] = x_ref[...].astype(F32).reshape(CHIPS * 8, 128)
+    part = [t_scr[pl.ds(i, CHIPS, stride=8), :] for i in range(8)]
     count = 2 * CHIPS
-
-    def tokens_of(kind):
-        rows = [
-            jnp.concatenate([part[kind * 8 + s * 4 + rr * 2], part[kind * 8 + s * 4 + rr * 2 + 1]], axis=1)
-            for rr in range(2)
-            for s in range(2)
-        ]
-        return jnp.concatenate(rows, axis=0)
-
-    tokens = tokens_of(0).astype(BF16)
+    rows = [
+        jnp.concatenate([part[s * 4 + rr * 2], part[s * 4 + rr * 2 + 1]], axis=1)
+        for rr in range(2)
+        for s in range(2)
+    ]
+    middle = jnp.concatenate(rows, axis=0)
+    tokens = standardize(middle).astype(BF16)
     q = matmul(tokens, wq_ref[...])
     k = matmul(tokens, wk_ref[...]).astype(BF16)
     v = matmul(tokens, wv_ref[...]).astype(BF16)
@@ -224,29 +219,29 @@
                 head_mask(attended.shape, h), out[h * count : (h + 1) * count], attended
             )
         gated.append((g[lo:hi] * attended).astype(BF16))
-    update = tokens_of(1) + matmul(jnp.concatenate(gated, axis=0), wo_ref[...])
+    result = middle + matmul(jnp.concatenate(gated, axis=0), wo_ref[...])
     for rr in range(2):
         for s in range(2):
             at = (rr * 2 + s) * CHIPS
             for half in range(2):
-                u_scr[pl.ds(s * CHIPS * 4 + rr * 2 + half, CHIPS, stride=4), :] = update[
+                t_scr[pl.ds(s * CHIPS * 4 + rr * 2 + half, CHIPS, stride=4), :] = result[
                     at : at + CHIPS, half * 128 : (half + 1) * 128
                 ]
-    out_ref[...] = u_scr[...].astype(BF16)
-
-
-def final_kernel(x_ref, rows_ref, out_ref, t_scr):
+    out_ref[...] = t_scr[...].astype(BF16)
+
+
+def final_kernel(x_ref, out_ref, t_scr):
     t_scr[...] = x_ref[...].astype(F32)
     part = [t_scr[pl.ds(s * CHIPS * 4 + i, CHIPS, stride=4), :] for s in range(2) for i in range(4)]
-    step = rows_ref.shape[0] // (2 * ZH)
+    step = out_ref.shape[0] // (2 * ZH)
     for s in range(2):
-        update = jnp.concatenate(
+        rows = jnp.concatenate(
             [jnp.concatenate([part[s * 4 + rr * 2], part[s * 4 + rr * 2 + 1]], axis=1) for rr in range(2)],
             axis=0,
         )
         for z in range(ZH):
             at = (z * 2 + s) * step
-            out_ref[at : at + step] = rows_ref[at : at + step] + update[z * step : (z + 1) * step]
+            out_ref[at : at + step] = rows[z * step : (z + 1) * step]
 
 
 def shards(
@@ -321,7 +316,7 @@
     )
 
     block = lax.all_to_all(send, ("zh", "y"), 0, 0, tiled=True)
-    update = call(
+    result = call(
         column_kernel,
         jax.ShapeDtypeStruct((CHIPS * 8, 128), BF16),
         block,
@@ -330,14 +325,13 @@
         col_wv,
         col_wg,
         col_wo,
-        scratch=[pltpu.VMEM((CHIPS * 16, 128), F32), pltpu.VMEM((CHIPS * 8, 128), F32)],
-    )
-    back = lax.all_to_all(update.reshape(2 * CHIPS, 4, 128), ("c", "zh", "y"), 0, 0, tiled=True)
+        scratch=[pltpu.VMEM((CHIPS * 8, 128), F32)],
+    )
+    back = lax.all_to_all(result.reshape(2 * CHIPS, 4, 128), ("c", "zh", "y"), 0, 0, tiled=True)
     out = call(
         final_kernel,
         jax.ShapeDtypeStruct((tokens, FEATURES), F32),
         back.reshape(CHIPS * 8, 128),
-        alignment[0],
         scratch=[pltpu.VMEM((CHIPS * 8, 128), F32)],
     )
     return out[None]

time: 99.4 us -> 99 us (level)
  no operation moved by 1% of the time
where the time goes in v4:
time: 99 us; the launch traced here: 98.3 us
  blocking collectives  55.6 us (56%)
  starting transfers between devices  28.8 us (29%)
  Pallas kernels  7.21 us (7%)
  waiting for transfers between devices  5.27 us (5%)
  local copies, waits for them, and re-layouts  1.28 us (1%)
    all_to_all x1, blocking collectives, shards(): block = lax.all_to_all(send, ('zh', 'y'), 0, 0, tiled=True)  20.1 us
    all_to_all x1, blocking collectives, shards(): lax.all_to_all(result.reshape(2 * CHIPS, 4, 128), ('c', 'zh', 'y'), 0, 0,...  19.3 us
    all_to_all x1, starting transfers between devices, shards(): wide = lax.all_to_all(wide, ('y', 'zh'), 0, 0, tiled=True)  13.2 us
    all_gather x1, blocking collectives, shards(): own_normed = lax.all_gather(near_normed, 'x', axis=0, tiled=True)  10.3 us
    ppermute x1, starting transfers between devices, shards(): bias = lax.ppermute(bias_here, ('y', 'zl', 'x'), turn)  8.28 us
    ppermute x1, starting transfers between devices, shards(): pair_normed = lax.ppermute(own_normed, 'c', swap)  7.26 us
    pallas_call x6, Pallas kernels, call(): pl.pallas_call(kernel, out_shape=out_shape, in_specs=[SMEM] * smem + [VME...  7.21 us
    all_to_all x1, waiting for transfers between devices, shards(): wide = lax.all_to_all(wide, ('y', 'zh'), 0, 0, tiled=True)  5.27 us
  transfers between devices with their start and end apart: 3, of which 1 were waited for; matrix products, arithmetic and copies ran while one was open for 0% of the time, Pallas kernels for 1%

profile of v4, /device:TPU:1, one launch (start us, length us, event | category | flops | bytes accessed | tf_op | source)
XLA Modules:
  0.0 98.3 jit_solution(15701779445446808659)
XLA Ops:
  0.0 2.2 %shard_map.129 = bf16[8,16,128]{2,1,0:T(8,128)(2,1)S(1)} custom-call(f32[8,128]{1,0:T(8,128)} %bitcast.12, f32[16,128,128]{2,1,0:T(8,128)} %x_ref.1), custom_call_target="tpu_custom_call" | custom-call | tf_op jit(solution)/shard_map/pallas_call | solution.py:32
  2.2 8.3 %collective-permute-start = (bf16[8,16,128]{2,1,0:T(8,128)(2,1)S(1)}, bf16[8,16,128]{2,1,0:T(8,128)(2,1)S(1)}, u32[]{:S(2)}, u32[]{:S(2)}) collective-permute-start(bf16[8,16,128]{2,1,0:T(8,128)(2,1)S(1)} %shard_map.129), channel_id=1, source_target_pairs={{0,256},{1,192},{2,64},{3,320},{4,448},{5,128},{6,0},{7,384},{64,1... | collective-permute-start | bytes 98312 | tf_op jit(solution)/shard_map/ppermute | solution.py:286
  10.5 0.0 copy-done
  10.5 0.2 shard_map.128
  10.7 3.8 %all_gather.10 = bf16[256,256]{1,0:T(8,128)(2,1)S(1)} all-gather(bf16[128,256]{1,0:T(8,128)(2,1)S(1)} %shard_map.128), channel_id=1, replica_groups=mesh['y'=8,'zh'=4,'c'=2,'zl'=2,'x'=4] {'zl'}, dimensions={0}, use_global_device_ids=true | all-gather | bytes 196608 | tf_op jit(solution)/shard_map/all_gather | solution.py:288
  14.5 0.0 collective-permute-done
  14.5 1.2 %broadcast_in_dim.4 = bf16[32,8,16,128]{3,2,1,0:T(8,128)(2,1)} broadcast(bf16[8,16,128]{2,1,0:T(8,128)(2,1)S(1)} %collective-permute-done), dimensions={1,2,3} | broadcast | bytes 1081344 | tf_op jit(solution)/shard_map/broadcast_in_dim | solution.py:295
  15.7 13.2 %all-to-all-start = ((bf16[32,8,16,128]{3,2,1,0:T(8,128)(2,1)}), bf16[32,8,16,128]{3,2,1,0:T(8,128)(2,1)S(1)}, u32[]{:S(2)}, u32[]{:S(2)}) async-start(bf16[32,8,16,128]{3,2,1,0:T(8,128)(2,1)} %broadcast_in_dim.4), calls=%async_computation | async-start | bytes 2097152 | tf_op jit(solution)/shard_map/all_to_all | solution.py:296
  28.9 10.3 %all_gather.11.own_ref = bf16[1024,256]{1,0:T(8,128)(2,1)S(1)} all-gather(bf16[256,256]{1,0:T(8,128)(2,1)S(1)} %all_gather.10), channel_id=1, replica_groups=mesh['y'=8,'zh'=4,'c'=2,'zl'=2,'x'=4] {'x'}, dimensions={0}, use_global_device_ids=true | all-gather | bytes 655360 | tf_op jit(solution)/shard_map/all_gather | solution.py:290
  39.3 7.3 %collective-permute-start.1 = (bf16[1024,256]{1,0:T(8,128)(2,1)S(1)}, bf16[1024,256]{1,0:T(8,128)(2,1)S(1)}, u32[]{:S(2)}, u32[]{:S(2)}) collective-permute-start(bf16[1024,256]{1,0:T(8,128)(2,1)S(1)} %all_gather.11.own_ref), channel_id=1, source_target_pairs={{0,8},{8,0},{1,9},{9,1},{2,10},{10,2},{3,11},{11,3},{4,12},{12,4},... | collective-permute-start | bytes 1572872 | tf_op jit(solution)/shard_map/ppermute | solution.py:291
  46.6 0.0 copy-start.1
  46.6 0.0 copy-start.2
  46.6 2.1 %all_gather.9 = f32[2,128,256]{2,1,0:T(8,128)S(1)} all-gather(f32[1,128,256]{2,1,0:T(8,128)S(1)} %copy-done), channel_id=1, replica_groups=mesh['y'=8,'zh'=4,'c'=2,'zl'=2,'x'=4] {'c'}, dimensions={0}, use_global_device_ids=true | all-gather | bytes 393216 | tf_op jit(solution)/shard_map/all_gather | solution.py:292
  48.7 0.0 copy-done.1
  48.7 0.0 copy-done.2
  48.7 0.0 copy-start.10
  48.7 0.3 shard_map.127
  49.1 0.0 collective-permute-done.1.pair_ref
  49.1 5.3 %all-to-all-done.bias_ref = bf16[32,8,16,128]{3,2,1,0:T(8,128)(2,1)S(1)} async-done(((bf16[32,8,16,128]{3,2,1,0:T(8,128)(2,1)}), bf16[32,8,16,128]{3,2,1,0:T(8,128)(2,1)S(1)}, u32[]{:S(2)}, u32[]{:S(2)}) %all-to-all-start) | async-done | bytes 1048608 | tf_op jit(solution)/shard_map/all_to_all | solution.py:296
  54.4 0.0 copy-done.8
  54.4 0.0 copy-done.10
  54.4 0.0 copy-start.4
  54.4 0.0 copy-start.5
  54.4 0.0 copy-start.6
  54.4 0.0 copy-start.7
  54.4 2.8 %shard_map.130 = bf16[32,8,128]{2,1,0:T(8,128)(2,1)S(1)} custom-call(s32[1]{0:T(128)} %bitcast.c_ref, s32[1]{0:T(128)} %bitcast.1.here_ref, bf16[2,64,256]{2,1,0:T(8,128)(2,1)S(1)} %get-tuple-element.10.q_ref, bf16[1024,256]{1,0:T(8,128)(2,1)S(1)} %all_gather.11.own_ref, bf16[1024,256]{1,0:T(8,128)(2,1)S(1)} %collective-permute-done.1.pair_ref, ...), custom_call_target="tpu_custom_call" | custom-call | flops 1073741824 | bytes 6291456 | tf_op jit(solution)/shard_map/pallas_call | solution.py:32
  57.2 0.0 copy-start.3
  57.2 20.1 %all_to_all.15.x_ref = bf16[32,8,128]{2,1,0:T(8,128)(2,1)S(1)} all-to-all(bf16[32,8,128]{2,1,0:T(8,128)(2,1)S(1)} %shard_map.130), channel_id=1, replica_groups=mesh['y'=8,'zh'=4,'c'=2,'zl'=2,'x'=4] {'zh','y'}, dimensions={0} | all-to-all | bytes 131072 | tf_op jit(solution)/shard_map/all_to_all | solution.py:318
  77.3 0.0 copy-done.6
  77.3 1.1 %shard_map.131 = bf16[256,128]{1,0:T(8,128)(2,1)S(1)} custom-call(bf16[32,8,128]{2,1,0:T(8,128)(2,1)S(1)} %all_to_all.15.x_ref, bf16[256,256]{1,0:T(8,128)(2,1)S(1)} %copy-done.3, bf16[256,256]{1,0:T(8,128)(2,1)S(1)} %copy-done.4, bf16[256,256]{1,0:T(8,128)(2,1)S(1)} %copy-done.5, bf16[256,256]{1,0:T(8,128)(2,1)S(1)} %copy-done.6, bf16[256,256]{1,0:T(8,128)(2,1)S(1)} %copy-done.7), custom_call_target="tpu_custom_call" | custom-call | tf_op jit(solution)/shard_map/pallas_call | solution.py:32
  78.3 19.3 %all_to_all.16 = bf16[64,4,128]{2,1,0:T(4,128)(2,1)S(1)} all-to-all(bf16[64,4,128]{2,1,0:T(4,128)(2,1)S(1)} %bitcast.10), channel_id=1, replica_groups=mesh['y'=8,'zh'=4,'c'=2,'zl'=2,'x'=4] {'c','zh','y'}, dimensions={0} | all-to-all | bytes 131072 | tf_op jit(solution)/shard_map/all_to_all | solution.py:330
  97.6 0.7 shard_map.132
  (8 shorter events, 0.0 us)
Async XLA Ops:
  0.0 10.5 %copy-start = (f32[1,128,256]{2,1,0:T(8,128)S(1)}, f32[1,128,256]{2,1,0:T(8,128)}, u32[]{:S(2)}) copy-start(f32[1,128,256]{2,1,0:T(8,128)} %param.13) | copy-start | bytes 393220
  2.2 12.3 %collective-permute-start = (bf16[8,16,128]{2,1,0:T(8,128)(2,1)S(1)}, bf16[8,16,128]{2,1,0:T(8,128)(2,1)S(1)}, u32[]{:S(2)}, u32[]{:S(2)}) collective-permute-start(bf16[8,16,128]{2,1,0:T(8,128)(2,1)S(1)} %shard_map.129), channel_id=1, source_target_pairs={{0,256},{1,192},{2,64},{3,320},{4,448},{5,128},{6,0},{7,384},{64,1... | collective-permute-start | bytes 98312 | tf_op jit(solution)/shard_map/ppermute | solution.py:286
  15.7 38.7 %all-to-all-start = ((bf16[32,8,16,128]{3,2,1,0:T(8,128)(2,1)}), bf16[32,8,16,128]{3,2,1,0:T(8,128)(2,1)S(1)}, u32[]{:S(2)}, u32[]{:S(2)}) async-start(bf16[32,8,16,128]{3,2,1,0:T(8,128)(2,1)} %broadcast_in_dim.4), calls=%async_computation | async-start | bytes 2097152 | tf_op jit(solution)/shard_map/all_to_all | solution.py:296
  39.3 9.8 %collective-permute-start.1 = (bf16[1024,256]{1,0:T(8,128)(2,1)S(1)}, bf16[1024,256]{1,0:T(8,128)(2,1)S(1)}, u32[]{:S(2)}, u32[]{:S(2)}) collective-permute-start(bf16[1024,256]{1,0:T(8,128)(2,1)S(1)} %all_gather.11.own_ref), channel_id=1, source_target_pairs={{0,8},{8,0},{1,9},{9,1},{2,10},{10,2},{3,11},{11,3},{4,12},{12,4},... | collective-permute-start | bytes 1572872 | tf_op jit(solution)/shard_map/ppermute | solution.py:291
  46.6 2.2 %copy-start.1 = (bf16[256,256]{1,0:T(8,128)(2,1)S(1)}, bf16[256,256]{1,0:T(8,128)(2,1)}, u32[]{:S(2)}) copy-start(bf16[256,256]{1,0:T(8,128)(2,1)} %wq_ref.2) | copy-start | bytes 393220
  46.6 2.1 %copy-start.2 = (bf16[256,256]{1,0:T(8,128)(2,1)S(1)}, bf16[256,256]{1,0:T(8,128)(2,1)}, u32[]{:S(2)}) copy-start(bf16[256,256]{1,0:T(8,128)(2,1)} %wg_ref.2) | copy-start | bytes 393220
  48.7 5.6 %copy-start.8 = (bf16[256,256]{1,0:T(8,128)(2,1)S(1)}, bf16[256,256]{1,0:T(8,128)(2,1)}, u32[]{:S(2)}) copy-start(bf16[256,256]{1,0:T(8,128)(2,1)} %wk_ref.2) | copy-start | bytes 393220
  48.7 5.6 %copy-start.9 = (bf16[256,256]{1,0:T(8,128)(2,1)S(1)}, bf16[256,256]{1,0:T(8,128)(2,1)}, u32[]{:S(2)}) copy-start(bf16[256,256]{1,0:T(8,128)(2,1)} %wv_ref.2) | copy-start | bytes 393220
  48.7 5.6 %copy-start.10 = (bf16[256,256]{1,0:T(8,128)(2,1)S(1)}, bf16[256,256]{1,0:T(8,128)(2,1)}, u32[]{:S(2)}) copy-start(bf16[256,256]{1,0:T(8,128)(2,1)} %wo_ref.2) | copy-start | bytes 393220
  54.4 22.9 %copy-start.4 = (bf16[256,256]{1,0:T(8,128)(2,1)S(1)}, bf16[256,256]{1,0:T(8,128)(2,1)}, u32[]{:S(2)}) copy-start(bf16[256,256]{1,0:T(8,128)(2,1)} %wk_ref.3) | copy-start | bytes 393220
  54.4 22.9 %copy-start.5 = (bf16[256,256]{1,0:T(8,128)(2,1)S(1)}, bf16[256,256]{1,0:T(8,128)(2,1)}, u32[]{:S(2)}) copy-start(bf16[256,256]{1,0:T(8,128)(2,1)} %wv_ref.3) | copy-start | bytes 393220
  54.4 22.9 %copy-start.6 = (bf16[256,256]{1,0:T(8,128)(2,1)S(1)}, bf16[256,256]{1,0:T(8,128)(2,1)}, u32[]{:S(2)}) copy-start(bf16[256,256]{1,0:T(8,128)(2,1)} %wg_ref.3) | copy-start | bytes 393220
  54.4 22.9 %copy-start.7 = (bf16[256,256]{1,0:T(8,128)(2,1)S(1)}, bf16[256,256]{1,0:T(8,128)(2,1)}, u32[]{:S(2)}) copy-start(bf16[256,256]{1,0:T(8,128)(2,1)} %wo_ref.3) | copy-start | bytes 393220
  57.2 20.1 %copy-start.3 = (bf16[256,256]{1,0:T(8,128)(2,1)S(1)}, bf16[256,256]{1,0:T(8,128)(2,1)}, u32[]{:S(2)}) copy-start(bf16[256,256]{1,0:T(8,128)(2,1)} %wq_ref.3) | copy-start | bytes 393220

commit v5 on v3

--- a/solution.py
+++ b/solution.py
@@ -60,13 +60,13 @@
     count = x_ref.shape[0]
     parts = sems.shape[0] - 1
     step = count // parts
-    first = pltpu.make_async_copy(w_hbm, w_ref, sems.at[parts])
-    first.start()
     copies = []
     for n in range(parts):
         part = pl.ds(n * step, step)
         copies.append(pltpu.make_async_copy(x_ref.at[part], x_scr.at[part], sems.at[n]))
         copies[n].start()
+    first = pltpu.make_async_copy(w_hbm, w_ref, sems.at[parts])
+    first.start()
     first.wait()
     w = w_ref[...]
     wh = w.astype(BF16)
@@ -74,9 +74,9 @@
     top = jnp.concatenate([wh.astype(F32), wh.astype(F32)], axis=1)
     low = jnp.concatenate([wl.astype(F32), jnp.zeros_like(w)], axis=1)
     weights = jnp.concatenate([top, low], axis=0).astype(BF16)
+    for copy in copies:
+        copy.wait()
     for i in range(count):
-        if i % step == 0:
-            copies[i // step].wait()
         d = standardize(x_scr[i])
         dh = d.astype(BF16)
         dl = (d - dh.astype(F32)).astype(BF16)
@@ -130,7 +130,7 @@
                 p_scr[s, lo:hi, n * cols : (n + 1) * cols] = e.astype(BF16)
             shares.append(1.0 / jnp.sum(total, axis=-1, keepdims=True))
 
-    for s, ref in enumerate((own_ref, pair_ref)):
+    def prepare(s, ref):
         tokens = ref[...]
         k = matmul(tokens, wk_ref[...]).astype(BF16)
         v_scr[s] = matmul(tokens, wv_ref[...]).astype(BF16)
@@ -138,9 +138,13 @@
         masked = [jnp.where(head_mask(q.shape, h), q, 0.0).astype(BF16) for h in range(HEADS)]
         masked = jnp.concatenate(masked, axis=0)
         s_scr[s] = lax.dot_general(masked, k, NT, preferred_element_type=F32)
-    for s in range(2):
-        softmax(s)
-        outs.append(matmul(p_scr[s], v_scr[s]))
+
+    prepare(0, own_ref)
+    softmax(0)
+    prepare(1, pair_ref)
+    outs.append(matmul(p_scr[0], v_scr[0]))
+    softmax(1)
+    outs.append(matmul(p_scr[1], v_scr[1]))
     for s in range(2):
         attended = jnp.zeros((count, FEATURES), F32)
         for h in range(HEADS):
@@ -285,7 +289,7 @@
             pltpu.VMEM((HEADS, pair_shape[2]), F32),
             pltpu.VMEM(pair_shape, F32),
             pltpu.VMEM(bias_shape, F32),
-            pltpu.SemaphoreType.DMA((2,)),
+            pltpu.SemaphoreType.DMA((3,)),
         ],
     )
     bias = lax.ppermute(bias_here, ("y", "zl", "x"), turn)

time: 99.4 us -> 99.4 us (level)
  no operation moved by 1% of the time
where the time goes in v5:
time: 99.4 us; the launch traced here: 98.6 us
  blocking collectives  55.9 us (56%)
  starting transfers between devices  28.8 us (29%)
  Pallas kernels  7.21 us (7%)
  waiting for transfers between devices  5.27 us (5%)
  local copies, waits for them, and re-layouts  1.28 us (1%)
    all_to_all x1, blocking collectives, shards(): block = lax.all_to_all(send, ('zh', 'y'), 0, 0, tiled=True)  20.4 us
    all_to_all x1, blocking collectives, shards(): lax.all_to_all(update.reshape(2 * CHIPS, 4, 128), ('c', 'zh', 'y'), 0, 0,...  19.3 us
    all_to_all x1, starting transfers between devices, shards(): wide = lax.all_to_all(wide, ('y', 'zh'), 0, 0, tiled=True)  13.2 us
    all_gather x1, blocking collectives, shards(): own_normed = lax.all_gather(near_normed, 'x', axis=0, tiled=True)  10.3 us
    ppermute x1, starting transfers between devices, shards(): bias = lax.ppermute(bias_here, ('y', 'zl', 'x'), turn)  8.28 us
    ppermute x1, starting transfers between devices, shards(): pair_normed = lax.ppermute(own_normed, 'c', swap)  7.26 us
    pallas_call x6, Pallas kernels, call(): pl.pallas_call(kernel, out_shape=out_shape, in_specs=[SMEM] * smem + [VME...  7.21 us
    all_to_all x1, waiting for transfers between devices, shards(): wide = lax.all_to_all(wide, ('y', 'zh'), 0, 0, tiled=True)  5.27 us
  transfers between devices with their start and end apart: 3, of which 1 were waited for; matrix products, arithmetic and copies ran while one was open for 0% of the time, Pallas kernels for 1%

profile of v5, /device:TPU:1, one launch (start us, length us, event | category | flops | bytes accessed | tf_op | source)
XLA Modules:
  0.0 98.6 jit_solution(5353102756465179050)
XLA Ops:
  0.0 2.2 %shard_map.129 = bf16[8,16,128]{2,1,0:T(8,128)(2,1)S(1)} custom-call(f32[8,128]{1,0:T(8,128)} %bitcast.13, f32[16,128,128]{2,1,0:T(8,128)} %x_ref.1), custom_call_target="tpu_custom_call" | custom-call | tf_op jit(solution)/shard_map/pallas_call | solution.py:32
  2.2 8.3 %collective-permute-start = (bf16[8,16,128]{2,1,0:T(8,128)(2,1)S(1)}, bf16[8,16,128]{2,1,0:T(8,128)(2,1)S(1)}, u32[]{:S(2)}, u32[]{:S(2)}) collective-permute-start(bf16[8,16,128]{2,1,0:T(8,128)(2,1)S(1)} %shard_map.129), channel_id=1, source_target_pairs={{0,256},{1,192},{2,64},{3,320},{4,448},{5,128},{6,0},{7,384},{64,1... | collective-permute-start | bytes 98312 | tf_op jit(solution)/shard_map/ppermute | solution.py:295
  10.5 0.0 copy-done
  10.5 0.2 shard_map.128
  10.7 3.8 %all_gather.10 = bf16[256,256]{1,0:T(8,128)(2,1)S(1)} all-gather(bf16[128,256]{1,0:T(8,128)(2,1)S(1)} %shard_map.128), channel_id=1, replica_groups=mesh['y'=8,'zh'=4,'c'=2,'zl'=2,'x'=4] {'zl'}, dimensions={0}, use_global_device_ids=true | all-gather | bytes 196608 | tf_op jit(solution)/shard_map/all_gather | solution.py:297
  14.5 0.0 collective-permute-done
  14.5 1.2 %broadcast_in_dim.4 = bf16[32,8,16,128]{3,2,1,0:T(8,128)(2,1)} broadcast(bf16[8,16,128]{2,1,0:T(8,128)(2,1)S(1)} %collective-permute-done), dimensions={1,2,3} | broadcast | bytes 1081344 | tf_op jit(solution)/shard_map/broadcast_in_dim | solution.py:304
  15.7 13.2 %all-to-all-start = ((bf16[32,8,16,128]{3,2,1,0:T(8,128)(2,1)}), bf16[32,8,16,128]{3,2,1,0:T(8,128)(2,1)S(1)}, u32[]{:S(2)}, u32[]{:S(2)}) async-start(bf16[32,8,16,128]{3,2,1,0:T(8,128)(2,1)} %broadcast_in_dim.4), calls=%async_computation | async-start | bytes 2097152 | tf_op jit(solution)/shard_map/all_to_all | solution.py:305
  28.9 10.3 %all_gather.11.own_ref = bf16[1024,256]{1,0:T(8,128)(2,1)S(1)} all-gather(bf16[256,256]{1,0:T(8,128)(2,1)S(1)} %all_gather.10), channel_id=1, replica_groups=mesh['y'=8,'zh'=4,'c'=2,'zl'=2,'x'=4] {'x'}, dimensions={0}, use_global_device_ids=true | all-gather | bytes 655360 | tf_op jit(solution)/shard_map/all_gather | solution.py:299
  39.3 7.3 %collective-permute-start.1 = (bf16[1024,256]{1,0:T(8,128)(2,1)S(1)}, bf16[1024,256]{1,0:T(8,128)(2,1)S(1)}, u32[]{:S(2)}, u32[]{:S(2)}) collective-permute-start(bf16[1024,256]{1,0:T(8,128)(2,1)S(1)} %all_gather.11.own_ref), channel_id=1, source_target_pairs={{0,8},{8,0},{1,9},{9,1},{2,10},{10,2},{3,11},{11,3},{4,12},{12,4},... | collective-permute-start | bytes 1572872 | tf_op jit(solution)/shard_map/ppermute | solution.py:300
  46.5 0.0 copy-start.1
  46.5 0.0 copy-start.2
  46.6 2.1 %all_gather.9 = f32[2,128,256]{2,1,0:T(8,128)S(1)} all-gather(f32[1,128,256]{2,1,0:T(8,128)S(1)} %copy-done), channel_id=1, replica_groups=mesh['y'=8,'zh'=4,'c'=2,'zl'=2,'x'=4] {'c'}, dimensions={0}, use_global_device_ids=true | all-gather | bytes 393216 | tf_op jit(solution)/shard_map/all_gather | solution.py:301
  48.7 0.0 copy-done.1
  48.7 0.0 copy-done.2
  48.7 0.0 copy-start.10
  48.7 0.3 shard_map.127
  49.0 0.0 collective-permute-done.1.pair_ref
  49.1 5.3 %all-to-all-done.bias_ref = bf16[32,8,16,128]{3,2,1,0:T(8,128)(2,1)S(1)} async-done(((bf16[32,8,16,128]{3,2,1,0:T(8,128)(2,1)}), bf16[32,8,16,128]{3,2,1,0:T(8,128)(2,1)S(1)}, u32[]{:S(2)}, u32[]{:S(2)}) %all-to-all-start) | async-done | bytes 1048608 | tf_op jit(solution)/shard_map/all_to_all | solution.py:305
  54.3 0.0 copy-done.8
  54.3 0.0 copy-done.9
  54.3 0.0 copy-start.5
  54.4 0.0 copy-start.6
  54.4 0.0 copy-start.7
  54.4 2.9 %shard_map.130 = bf16[32,16,128]{2,1,0:T(8,128)(2,1)S(1)} custom-call(s32[1]{0:T(128)} %bitcast.c_ref, s32[1]{0:T(128)} %bitcast.1.here_ref, bf16[2,64,256]{2,1,0:T(8,128)(2,1)S(1)} %get-tuple-element.10.q_ref, bf16[1024,256]{1,0:T(8,128)(2,1)S(1)} %all_gather.11.own_ref, bf16[1024,256]{1,0:T(8,128)(2,1)S(1)} %collective-permute-done.1.pair_ref, ...), custom_call_target="tpu_custom_call" | custom-call | flops 1073741824 | bytes 6291456 | tf_op jit(solution)/shard_map/pallas_call | solution.py:32
  57.3 0.0 copy-start.3
  57.3 0.0 copy-start.4
  57.3 20.4 %all_to_all.15.x_ref = bf16[32,16,128]{2,1,0:T(8,128)(2,1)S(1)} all-to-all(bf16[32,16,128]{2,1,0:T(8,128)(2,1)S(1)} %shard_map.130), channel_id=1, replica_groups=mesh['y'=8,'zh'=4,'c'=2,'zl'=2,'x'=4] {'zh','y'}, dimensions={0} | all-to-all | bytes 262144 | tf_op jit(solution)/shard_map/all_to_all | solution.py:327
  77.7 0.0 copy-done.6
  77.8 0.9 shard_map.131
  78.7 19.3 %all_to_all.16 = bf16[64,4,128]{2,1,0:T(4,128)(2,1)S(1)} all-to-all(bf16[64,4,128]{2,1,0:T(4,128)(2,1)S(1)} %bitcast.12), channel_id=1, replica_groups=mesh['y'=8,'zh'=4,'c'=2,'zl'=2,'x'=4] {'c','zh','y'}, dimensions={0} | all-to-all | bytes 131072 | tf_op jit(solution)/shard_map/all_to_all | solution.py:339
  98.0 0.7 shard_map.132
  (8 shorter events, 0.0 us)
Async XLA Ops:
  0.0 10.5 %copy-start = (f32[1,128,256]{2,1,0:T(8,128)S(1)}, f32[1,128,256]{2,1,0:T(8,128)}, u32[]{:S(2)}) copy-start(f32[1,128,256]{2,1,0:T(8,128)} %param.13) | copy-start | bytes 393220
  2.2 12.3 %collective-permute-start = (bf16[8,16,128]{2,1,0:T(8,128)(2,1)S(1)}, bf16[8,16,128]{2,1,0:T(8,128)(2,1)S(1)}, u32[]{:S(2)}, u32[]{:S(2)}) collective-permute-start(bf16[8,16,128]{2,1,0:T(8,128)(2,1)S(1)} %shard_map.129), channel_id=1, source_target_pairs={{0,256},{1,192},{2,64},{3,320},{4,448},{5,128},{6,0},{7,384},{64,1... | collective-permute-start | bytes 98312 | tf_op jit(solution)/shard_map/ppermute | solution.py:295
  15.7 38.7 %all-to-all-start = ((bf16[32,8,16,128]{3,2,1,0:T(8,128)(2,1)}), bf16[32,8,16,128]{3,2,1,0:T(8,128)(2,1)S(1)}, u32[]{:S(2)}, u32[]{:S(2)}) async-start(bf16[32,8,16,128]{3,2,1,0:T(8,128)(2,1)} %broadcast_in_dim.4), calls=%async_computation | async-start | bytes 2097152 | tf_op jit(solution)/shard_map/all_to_all | solution.py:305
  39.3 9.8 %collective-permute-start.1 = (bf16[1024,256]{1,0:T(8,128)(2,1)S(1)}, bf16[1024,256]{1,0:T(8,128)(2,1)S(1)}, u32[]{:S(2)}, u32[]{:S(2)}) collective-permute-start(bf16[1024,256]{1,0:T(8,128)(2,1)S(1)} %all_gather.11.own_ref), channel_id=1, source_target_pairs={{0,8},{8,0},{1,9},{9,1},{2,10},{10,2},{3,11},{11,3},{4,12},{12,4},... | collective-permute-start | bytes 1572872 | tf_op jit(solution)/shard_map/ppermute | solution.py:300
  46.5 2.2 %copy-start.1 = (bf16[256,256]{1,0:T(8,128)(2,1)S(1)}, bf16[256,256]{1,0:T(8,128)(2,1)}, u32[]{:S(2)}) copy-start(bf16[256,256]{1,0:T(8,128)(2,1)} %wq_ref.2) | copy-start | bytes 393220
  46.5 2.1 %copy-start.2 = (bf16[256,256]{1,0:T(8,128)(2,1)S(1)}, bf16[256,256]{1,0:T(8,128)(2,1)}, u32[]{:S(2)}) copy-start(bf16[256,256]{1,0:T(8,128)(2,1)} %wg_ref.2) | copy-start | bytes 393220
  48.7 5.6 %copy-start.8 = (bf16[256,256]{1,0:T(8,128)(2,1)S(1)}, bf16[256,256]{1,0:T(8,128)(2,1)}, u32[]{:S(2)}) copy-start(bf16[256,256]{1,0:T(8,128)(2,1)} %wk_ref.2) | copy-start | bytes 393220
  48.7 5.6 %copy-start.9 = (bf16[256,256]{1,0:T(8,128)(2,1)S(1)}, bf16[256,256]{1,0:T(8,128)(2,1)}, u32[]{:S(2)}) copy-start(bf16[256,256]{1,0:T(8,128)(2,1)} %wv_ref.2) | copy-start | bytes 393220
  48.7 5.6 %copy-start.10 = (bf16[256,256]{1,0:T(8,128)(2,1)S(1)}, bf16[256,256]{1,0:T(8,128)(2,1)}, u32[]{:S(2)}) copy-start(bf16[256,256]{1,0:T(8,128)(2,1)} %wo_ref.2) | copy-start | bytes 393220
  54.3 23.4 %copy-start.5 = (bf16[256,256]{1,0:T(8,128)(2,1)S(1)}, bf16[256,256]{1,0:T(8,128)(2,1)}, u32[]{:S(2)}) copy-start(bf16[256,256]{1,0:T(8,128)(2,1)} %wv_ref.3) | copy-start | bytes 393220
  54.4 23.4 %copy-start.6 = (bf16[256,256]{1,0:T(8,128)(2,1)S(1)}, bf16[256,256]{1,0:T(8,128)(2,1)}, u32[]{:S(2)}) copy-start(bf16[256,256]{1,0:T(8,128)(2,1)} %wg_ref.3) | copy-start | bytes 393220
  54.4 23.4 %copy-start.7 = (bf16[256,256]{1,0:T(8,128)(2,1)S(1)}, bf16[256,256]{1,0:T(8,128)(2,1)}, u32[]{:S(2)}) copy-start(bf16[256,256]{1,0:T(8,128)(2,1)} %wo_ref.3) | copy-start | bytes 393220
  57.3 20.4 %copy-start.3 = (bf16[256,256]{1,0:T(8,128)(2,1)S(1)}, bf16[256,256]{1,0:T(8,128)(2,1)}, u32[]{:S(2)}) copy-start(bf16[256,256]{1,0:T(8,128)(2,1)} %wq_ref.3) | copy-start | bytes 393220
  57.3 20.4 %copy-start.4 = (bf16[256,256]{1,0:T(8,128)(2,1)S(1)}, bf16[256,256]{1,0:T(8,128)(2,1)}, u32[]{:S(2)}) copy-start(bf16[256,256]{1,0:T(8,128)(2,1)} %wk_ref.3) | copy-start | bytes 393220

commit v6 on v5

--- a/solution.py
+++ b/solution.py
@@ -17,7 +17,7 @@
 RES = ("zl", "x")
 CHIPS = Y * ZH
 BLOCKS = ZL * X
-TURN = (4, 3, 1, 5, 7, 2, 0, 6)
+TURN = (4, 2, 1, 3, 6, 5, 0, 7)
 TURN_BITS = sum(y << (4 * n) for n, y in enumerate(TURN))
 VMEM = pl.BlockSpec(memory_space=pltpu.VMEM)
 SMEM = pl.BlockSpec(memory_space=pltpu.SMEM)

time: 99.4 us -> 99.7 us (level)
  no operation moved by 1% of the time
where the time goes in v6:
time: 99.7 us; the launch traced here: 98.3 us
  blocking collectives  56.1 us (56%)
  starting transfers between devices  28 us (28%)
  Pallas kernels  7.23 us (7%)
  waiting for transfers between devices  5.46 us (5%)
  local copies, waits for them, and re-layouts  1.28 us (1%)
    all_to_all x1, blocking collectives, shards(): block = lax.all_to_all(send, ('zh', 'y'), 0, 0, tiled=True)  20.4 us
    all_to_all x1, blocking collectives, shards(): lax.all_to_all(update.reshape(2 * CHIPS, 4, 128), ('c', 'zh', 'y'), 0, 0,...  19 us
    all_to_all x1, starting transfers between devices, shards(): wide = lax.all_to_all(wide, ('y', 'zh'), 0, 0, tiled=True)  13 us
    all_gather x1, blocking collectives, shards(): own_normed = lax.all_gather(near_normed, 'x', axis=0, tiled=True)  10.8 us
    ppermute x1, starting transfers between devices, shards(): bias = lax.ppermute(bias_here, ('y', 'zl', 'x'), turn)  8.28 us
    pallas_call x6, Pallas kernels, call(): pl.pallas_call(kernel, out_shape=out_shape, in_specs=[SMEM] * smem + [VME...  7.23 us
    ppermute x1, starting transfers between devices, shards(): pair_normed = lax.ppermute(own_normed, 'c', swap)  6.73 us
    all_to_all x1, waiting for transfers between devices, shards(): wide = lax.all_to_all(wide, ('y', 'zh'), 0, 0, tiled=True)  5.46 us
  transfers between devices with their start and end apart: 3, of which 1 were waited for; matrix products, arithmetic and copies ran while one was open for 0% of the time, Pallas kernels for 1%

profile of v6, /device:TPU:1, one launch (start us, length us, event | category | flops | bytes accessed | tf_op | source)
XLA Modules:
  0.0 98.3 jit_solution(1895602891344681710)
XLA Ops:
  0.0 2.2 %shard_map.129 = bf16[8,16,128]{2,1,0:T(8,128)(2,1)S(1)} custom-call(f32[8,128]{1,0:T(8,128)} %bitcast.13, f32[16,128,128]{2,1,0:T(8,128)} %x_ref.1), custom_call_target="tpu_custom_call" | custom-call | tf_op jit(solution)/shard_map/pallas_call | solution.py:32
  2.2 8.3 %collective-permute-start = (bf16[8,16,128]{2,1,0:T(8,128)(2,1)S(1)}, bf16[8,16,128]{2,1,0:T(8,128)(2,1)S(1)}, u32[]{:S(2)}, u32[]{:S(2)}) collective-permute-start(bf16[8,16,128]{2,1,0:T(8,128)(2,1)S(1)} %shard_map.129), channel_id=1, source_target_pairs={{0,256},{1,128},{2,64},{3,192},{4,384},{5,320},{6,0},{7,448},{64,1... | collective-permute-start | bytes 98312 | tf_op jit(solution)/shard_map/ppermute | solution.py:295
  10.5 0.0 copy-done
  10.5 0.2 shard_map.128
  10.7 3.8 %all_gather.10 = bf16[256,256]{1,0:T(8,128)(2,1)S(1)} all-gather(bf16[128,256]{1,0:T(8,128)(2,1)S(1)} %shard_map.128), channel_id=1, replica_groups=mesh['y'=8,'zh'=4,'c'=2,'zl'=2,'x'=4] {'zl'}, dimensions={0}, use_global_device_ids=true | all-gather | bytes 196608 | tf_op jit(solution)/shard_map/all_gather | solution.py:297
  14.5 0.0 collective-permute-done
  14.5 1.2 %broadcast_in_dim.4 = bf16[32,8,16,128]{3,2,1,0:T(8,128)(2,1)} broadcast(bf16[8,16,128]{2,1,0:T(8,128)(2,1)S(1)} %collective-permute-done), dimensions={1,2,3} | broadcast | bytes 1081344 | tf_op jit(solution)/shard_map/broadcast_in_dim | solution.py:304
  15.7 13.0 %all-to-all-start = ((bf16[32,8,16,128]{3,2,1,0:T(8,128)(2,1)}), bf16[32,8,16,128]{3,2,1,0:T(8,128)(2,1)S(1)}, u32[]{:S(2)}, u32[]{:S(2)}) async-start(bf16[32,8,16,128]{3,2,1,0:T(8,128)(2,1)} %broadcast_in_dim.4), calls=%async_computation | async-start | bytes 2097152 | tf_op jit(solution)/shard_map/all_to_all | solution.py:305
  28.7 10.8 %all_gather.11.own_ref = bf16[1024,256]{1,0:T(8,128)(2,1)S(1)} all-gather(bf16[256,256]{1,0:T(8,128)(2,1)S(1)} %all_gather.10), channel_id=1, replica_groups=mesh['y'=8,'zh'=4,'c'=2,'zl'=2,'x'=4] {'x'}, dimensions={0}, use_global_device_ids=true | all-gather | bytes 655360 | tf_op jit(solution)/shard_map/all_gather | solution.py:299
  39.5 6.7 %collective-permute-start.1 = (bf16[1024,256]{1,0:T(8,128)(2,1)S(1)}, bf16[1024,256]{1,0:T(8,128)(2,1)S(1)}, u32[]{:S(2)}, u32[]{:S(2)}) collective-permute-start(bf16[1024,256]{1,0:T(8,128)(2,1)S(1)} %all_gather.11.own_ref), channel_id=1, source_target_pairs={{0,8},{8,0},{1,9},{9,1},{2,10},{10,2},{3,11},{11,3},{4,12},{12,4},... | collective-permute-start | bytes 1572872 | tf_op jit(solution)/shard_map/ppermute | solution.py:300
  46.3 0.0 copy-start.1
  46.3 0.0 copy-start.2
  46.3 2.1 %all_gather.9 = f32[2,128,256]{2,1,0:T(8,128)S(1)} all-gather(f32[1,128,256]{2,1,0:T(8,128)S(1)} %copy-done), channel_id=1, replica_groups=mesh['y'=8,'zh'=4,'c'=2,'zl'=2,'x'=4] {'c'}, dimensions={0}, use_global_device_ids=true | all-gather | bytes 393216 | tf_op jit(solution)/shard_map/all_gather | solution.py:301
  48.4 0.0 copy-done.1
  48.4 0.0 copy-start.10
  48.5 0.3 shard_map.127
  48.8 0.0 collective-permute-done.1.pair_ref
  48.8 5.5 %all-to-all-done.bias_ref = bf16[32,8,16,128]{3,2,1,0:T(8,128)(2,1)S(1)} async-done(((bf16[32,8,16,128]{3,2,1,0:T(8,128)(2,1)}), bf16[32,8,16,128]{3,2,1,0:T(8,128)(2,1)S(1)}, u32[]{:S(2)}, u32[]{:S(2)}) %all-to-all-start) | async-done | bytes 1048608 | tf_op jit(solution)/shard_map/all_to_all | solution.py:305
  54.3 0.0 copy-done.9
  54.3 0.0 copy-start.5
  54.3 0.0 copy-start.6
  54.3 0.0 copy-start.7
  54.3 3.0 %shard_map.130 = bf16[32,16,128]{2,1,0:T(8,128)(2,1)S(1)} custom-call(s32[1]{0:T(128)} %bitcast.c_ref, s32[1]{0:T(128)} %bitcast.1.here_ref, bf16[2,64,256]{2,1,0:T(8,128)(2,1)S(1)} %get-tuple-element.10.q_ref, bf16[1024,256]{1,0:T(8,128)(2,1)S(1)} %all_gather.11.own_ref, bf16[1024,256]{1,0:T(8,128)(2,1)S(1)} %collective-permute-done.1.pair_ref, ...), custom_call_target="tpu_custom_call" | custom-call | flops 1073741824 | bytes 6291456 | tf_op jit(solution)/shard_map/pallas_call | solution.py:32
  57.3 0.0 copy-start.3
  57.3 0.0 copy-start.4
  57.3 20.4 %all_to_all.15.x_ref = bf16[32,16,128]{2,1,0:T(8,128)(2,1)S(1)} all-to-all(bf16[32,16,128]{2,1,0:T(8,128)(2,1)S(1)} %shard_map.130), channel_id=1, replica_groups=mesh['y'=8,'zh'=4,'c'=2,'zl'=2,'x'=4] {'zh','y'}, dimensions={0} | all-to-all | bytes 262144 | tf_op jit(solution)/shard_map/all_to_all | solution.py:327
  77.7 0.0 copy-done.7
  77.7 0.0 copy-done.3
  77.7 0.0 copy-done.4
  77.7 0.9 shard_map.131
  78.6 19.0 %all_to_all.16 = bf16[64,4,128]{2,1,0:T(4,128)(2,1)S(1)} all-to-all(bf16[64,4,128]{2,1,0:T(4,128)(2,1)S(1)} %bitcast.12), channel_id=1, replica_groups=mesh['y'=8,'zh'=4,'c'=2,'zl'=2,'x'=4] {'c','zh','y'}, dimensions={0} | all-to-all | bytes 131072 | tf_op jit(solution)/shard_map/all_to_all | solution.py:339
  97.6 0.7 shard_map.132
  (8 shorter events, 0.0 us)
Async XLA Ops:
  0.0 10.5 %copy-start = (f32[1,128,256]{2,1,0:T(8,128)S(1)}, f32[1,128,256]{2,1,0:T(8,128)}, u32[]{:S(2)}) copy-start(f32[1,128,256]{2,1,0:T(8,128)} %param.13) | copy-start | bytes 393220
  2.2 12.3 %collective-permute-start = (bf16[8,16,128]{2,1,0:T(8,128)(2,1)S(1)}, bf16[8,16,128]{2,1,0:T(8,128)(2,1)S(1)}, u32[]{:S(2)}, u32[]{:S(2)}) collective-permute-start(bf16[8,16,128]{2,1,0:T(8,128)(2,1)S(1)} %shard_map.129), channel_id=1, source_target_pairs={{0,256},{1,128},{2,64},{3,192},{4,384},{5,320},{6,0},{7,448},{64,1... | collective-permute-start | bytes 98312 | tf_op jit(solution)/shard_map/ppermute | solution.py:295
  15.7 38.6 %all-to-all-start = ((bf16[32,8,16,128]{3,2,1,0:T(8,128)(2,1)}), bf16[32,8,16,128]{3,2,1,0:T(8,128)(2,1)S(1)}, u32[]{:S(2)}, u32[]{:S(2)}) async-start(bf16[32,8,16,128]{3,2,1,0:T(8,128)(2,1)} %broadcast_in_dim.4), calls=%async_computation | async-start | bytes 2097152 | tf_op jit(solution)/shard_map/all_to_all | solution.py:305
  39.5 9.3 %collective-permute-start.1 = (bf16[1024,256]{1,0:T(8,128)(2,1)S(1)}, bf16[1024,256]{1,0:T(8,128)(2,1)S(1)}, u32[]{:S(2)}, u32[]{:S(2)}) collective-permute-start(bf16[1024,256]{1,0:T(8,128)(2,1)S(1)} %all_gather.11.own_ref), channel_id=1, source_target_pairs={{0,8},{8,0},{1,9},{9,1},{2,10},{10,2},{3,11},{11,3},{4,12},{12,4},... | collective-permute-start | bytes 1572872 | tf_op jit(solution)/shard_map/ppermute | solution.py:300
  46.3 2.2 %copy-start.1 = (bf16[256,256]{1,0:T(8,128)(2,1)S(1)}, bf16[256,256]{1,0:T(8,128)(2,1)}, u32[]{:S(2)}) copy-start(bf16[256,256]{1,0:T(8,128)(2,1)} %wq_ref.2) | copy-start | bytes 393220
  46.3 2.1 %copy-start.2 = (bf16[256,256]{1,0:T(8,128)(2,1)S(1)}, bf16[256,256]{1,0:T(8,128)(2,1)}, u32[]{:S(2)}) copy-start(bf16[256,256]{1,0:T(8,128)(2,1)} %wg_ref.2) | copy-start | bytes 393220
  48.4 5.8 %copy-start.8 = (bf16[256,256]{1,0:T(8,128)(2,1)S(1)}, bf16[256,256]{1,0:T(8,128)(2,1)}, u32[]{:S(2)}) copy-start(bf16[256,256]{1,0:T(8,128)(2,1)} %wk_ref.2) | copy-start | bytes 393220
  48.4 5.8 %copy-start.9 = (bf16[256,256]{1,0:T(8,128)(2,1)S(1)}, bf16[256,256]{1,0:T(8,128)(2,1)}, u32[]{:S(2)}) copy-start(bf16[256,256]{1,0:T(8,128)(2,1)} %wv_ref.2) | copy-start | bytes 393220
  48.4 5.8 %copy-start.10 = (bf16[256,256]{1,0:T(8,128)(2,1)S(1)}, bf16[256,256]{1,0:T(8,128)(2,1)}, u32[]{:S(2)}) copy-start(bf16[256,256]{1,0:T(8,128)(2,1)} %wo_ref.2) | copy-start | bytes 393220
  54.3 23.4 %copy-start.5 = (bf16[256,256]{1,0:T(8,128)(2,1)S(1)}, bf16[256,256]{1,0:T(8,128)(2,1)}, u32[]{:S(2)}) copy-start(bf16[256,256]{1,0:T(8,128)(2,1)} %wv_ref.3) | copy-start | bytes 393220
  54.3 23.4 %copy-start.6 = (bf16[256,256]{1,0:T(8,128)(2,1)S(1)}, bf16[256,256]{1,0:T(8,128)(2,1)}, u32[]{:S(2)}) copy-start(bf16[256,256]{1,0:T(8,128)(2,1)} %wg_ref.3) | copy-start | bytes 393220
  54.3 23.4 %copy-start.7 = (bf16[256,256]{1,0:T(8,128)(2,1)S(1)}, bf16[256,256]{1,0:T(8,128)(2,1)}, u32[]{:S(2)}) copy-start(bf16[256,256]{1,0:T(8,128)(2,1)} %wo_ref.3) | copy-start | bytes 393220
  57.3 20.4 %copy-start.3 = (bf16[256,256]{1,0:T(8,128)(2,1)S(1)}, bf16[256,256]{1,0:T(8,128)(2,1)}, u32[]{:S(2)}) copy-start(bf16[256,256]{1,0:T(8,128)(2,1)} %wq_ref.3) | copy-start | bytes 393220
  57.3 20.4 %copy-start.4 = (bf16[256,256]{1,0:T(8,128)(2,1)S(1)}, bf16[256,256]{1,0:T(8,128)(2,1)}, u32[]{:S(2)}) copy-start(bf16[256,256]{1,0:T(8,128)(2,1)} %wk_ref.3) | copy-start | bytes 393220
